TPU v7x, 32 devices: a whole 2x2x4 slice. The times are simulated.
32 devices in a mesh: pipe: 4 (over y, core), expert: 8 (over z, x).
Axes of the slice: x: 2, y: 2, z: 4, core: 2. Of those that a mesh axis runs over, the one named last changes fastest.
Arguments:
- acts_first: bfloat16 [4, 1024, 3584], P('pipe', 'expert'), may hold values from -6 to 6
- route_first: int32 [4, 1024, 1], P('pipe', 'expert'), may hold values from 0 to 1; in each aligned block of 128 rows (0 to 127, 128 to 255, ..., all dimensions but the last counted through in order) at most 96 rows name the same one
- weight_first: float32 [4, 1024, 1], P('pipe', 'expert'), may hold values from 0.3 to 1.5
- acts_second: bfloat16 [4, 1024, 3584], P('pipe', 'expert'), may hold values from -6 to 6
- grad_second: bfloat16 [4, 1024, 3584], P('pipe', 'expert'), may hold values from -6 to 6
- route_second: int32 [4, 1024, 1], P('pipe', 'expert'), may hold values from 0 to 1; in each aligned block of 128 rows (0 to 127, 128 to 255, ..., all dimensions but the last counted through in order) at most 96 rows name the same one
- weight_second: float32 [4, 1024, 1], P('pipe', 'expert'), may hold values from 0.3 to 1.5
- gain_first: float32 [4, 3584], P('pipe'), may hold values from 0.5 to 1.5
- up_first: bfloat16 [4, 3584, 2048], P('pipe', None, 'expert'), may hold values from -0.09375 to 0.09375
- down_first: bfloat16 [4, 2048, 3584], P('pipe', 'expert'), may hold values from -0.1875 to 0.1875
- gain_second: float32 [4, 3584], P('pipe'), may hold values from 0.5 to 1.5
- up_second: bfloat16 [4, 3584, 2048], P('pipe', None, 'expert'), may hold values from -0.09375 to 0.09375
- down_second: bfloat16 [4, 2048, 3584], P('pipe', 'expert'), may hold values from -0.1875 to 0.1875
Outputs:
- next_first: bfloat16 [4, 1024, 3584], P('pipe', 'expert')
- next_grad: bfloat16 [4, 1024, 3584], P('pipe', 'expert')
Inputs may be any that keep to these rules, and one draw needn't show every extreme that they name: `route_first`: among the 128 tokens of one device (an aligned block of 128 tokens at one pipe index), at most 96 choose the same expert, and some device has exactly 96 on one expert. `route_second`: among the 128 tokens of one device (an aligned block of 128 tokens at one pipe index), at most 96 choose the same expert, and some device has exactly 96 on one expert.
All inputs are finite; a program needn't handle non-finite values.
Results may differ from a plain program's by a relative error of at most 0.0054.
Values may be sent and summed in bfloat16 or wider, within the bound.
No kernel may reach another device: no remote copies, remote signals or barrier semaphores. Data moves between devices by JAX's collectives and lax.ppermute only.
A program may use at most 128 MiB of HBM per device.

v0:
```python
import jax
import jax.numpy as jnp
from jax import lax
from jax.sharding import PartitionSpec as P

SPLIT = 4


def shifted(block, axis, distance):
    devices = range(lax.axis_size(axis))
    route = [((i - distance) % len(devices), i) for i in devices]
    return lax.ppermute(block, axis, route)


def normalize(acts, gain_row):
    values = acts.astype(jnp.float32)
    inverse_rms = lax.rsqrt(jnp.mean(values * values, axis=-1, keepdims=True) + 1e-06)
    return (values, inverse_rms, (values * inverse_rms * gain_row).astype(jnp.bfloat16))


def positions(route_ids, experts_count, capacity):
    onehot = (route_ids[:, None] == jnp.arange(experts_count, dtype=jnp.int32)[None, :]).astype(
        jnp.int32
    )
    before = jnp.cumsum(onehot, axis=0, dtype=jnp.int32) - onehot
    slot_index = jnp.sum(before * onehot, axis=1, dtype=jnp.int32)
    return route_ids * capacity + slot_index


def contract_last(left_rows, right_rows):
    return lax.dot_general(
        left_rows, right_rows, (((1,), (1,)), ((), ())), preferred_element_type=jnp.float32
    )


def per_device(
    acts_first,
    route_first,
    weight_first,
    acts_second,
    grad_second,
    route_second,
    weight_second,
    gain_first,
    up_first,
    down_first,
    gain_second,
    up_second,
    down_second,
):
    owners = lax.axis_size("expert")
    experts_count = owners // SPLIT
    tokens_here = acts_first.shape[1]
    model_width = acts_first.shape[2]
    capacity = 3 * tokens_here * SPLIT // (2 * owners)
    values_first, inverse_first, normed_first = normalize(acts_first[0], gain_first[0])
    values_second, inverse_second, normed_second = normalize(acts_second[0], gain_second[0])
    scaled_grad = (weight_second[0] * grad_second[0].astype(jnp.float32)).astype(jnp.bfloat16)
    where_first = positions(route_first[0, :, 0], experts_count, capacity)
    where_second = positions(route_second[0, :, 0], experts_count, capacity)
    outgoing = jnp.zeros((3, experts_count * capacity, model_width), jnp.bfloat16)
    outgoing = outgoing.at[0, where_first].set(normed_first)
    outgoing = outgoing.at[1, where_second].set(normed_second)
    outgoing = outgoing.at[2, where_second].set(scaled_grad)
    outgoing = outgoing.reshape(3, experts_count, capacity, model_width)
    copies = jnp.broadcast_to(
        outgoing[:, :, None], (3, experts_count, SPLIT, capacity, model_width)
    )
    copies = copies.reshape(3, owners, capacity, model_width)
    packed = lax.all_to_all(copies, "expert", split_axis=1, concat_axis=1, tiled=True)
    slot_total = packed.shape[1] * packed.shape[2]
    packed_rows = packed.reshape(3, slot_total, model_width)
    upper_first = jnp.dot(packed_rows[0], up_first[0], preferred_element_type=jnp.float32)
    hidden = jax.nn.silu(upper_first).astype(jnp.bfloat16)
    out_part = jnp.dot(hidden, down_first[0], preferred_element_type=jnp.float32).astype(
        jnp.bfloat16
    )
    upper_second = jnp.dot(packed_rows[1], up_second[0], preferred_element_type=jnp.float32)
    sigmoid_up = jax.nn.sigmoid(upper_second)
    back_hidden = contract_last(packed_rows[2], down_second[0])
    back_upper = (back_hidden * sigmoid_up * (1.0 + upper_second * (1.0 - sigmoid_up))).astype(
        jnp.bfloat16
    )
    back_part = contract_last(back_upper, up_second[0]).astype(jnp.bfloat16)
    result = jnp.stack([out_part, back_part]).reshape(
        2, packed.shape[1], packed.shape[2], model_width
    )
    returned = lax.all_to_all(result, "expert", split_axis=1, concat_axis=1, tiled=True)
    totals = jnp.sum(
        returned.reshape(2, experts_count, SPLIT, capacity, model_width), axis=2, dtype=jnp.float32
    )
    totals = totals.reshape(2, experts_count * capacity, model_width)
    expert_first = totals[0][where_first]
    back_normed = totals[1][where_second]
    mixed_first = (values_first + weight_first[0] * expert_first).astype(jnp.bfloat16)
    gained_back = gain_second[0] * back_normed
    scale_cubed = inverse_second * inverse_second * inverse_second
    grad_acts = (
        grad_second[0].astype(jnp.float32)
        + inverse_second * gained_back
        - values_second
        * scale_cubed
        * jnp.mean(values_second * gained_back, axis=-1, keepdims=True)
    )
    handed_on = shifted(jnp.stack([mixed_first, grad_acts.astype(jnp.bfloat16)]), "pipe", 1)
    return (handed_on[0][None], handed_on[1][None])


def solution(mesh):
    in_specs = (
        P("pipe", "expert", None),
        P("pipe", "expert", None),
        P("pipe", "expert", None),
        P("pipe", "expert", None),
        P("pipe", "expert", None),
        P("pipe", "expert", None),
        P("pipe", "expert", None),
        P("pipe", None),
        P("pipe", None, "expert"),
        P("pipe", "expert", None),
        P("pipe", None),
        P("pipe", None, "expert"),
        P("pipe", "expert", None),
    )
    out_specs = (P("pipe", "expert", None), P("pipe", "expert", None))
    return jax.shard_map(
        per_device, mesh=mesh, in_specs=in_specs, out_specs=out_specs, check_vma=False
    )
```

profile of v0, /device:TPU:0, one launch (start us, length us, event | category | flops | bytes accessed | tf_op | source)
XLA Modules:
  0.0 817.3 jit_solution(12612674498694052397)
XLA Ops:
  0.7 1.6 fusion.9
  8.6 1.5 fusion.5
  10.2 1.2 fusion.11
  13.8 2.2 broadcast_in_dim.6
  16.0 32.2 %scatter_fusion = bf16[3,192,3584]{2,1,0:T(8,128)(2,1)} fusion(bf16[3,192,3584]{2,1,0:T(8,128)(2,1)} %broadcast_in_dim.6, s32[128]{0:T(128)S(1)} %get-tuple-element.4, bf16[128,3584]{1,0:T(8,128)(2,1)} %fusion.7), kind=kCustom, calls=%fused_computation.2 | custom fusion | bytes 2753536 | tf_op jit(solution)/shard_map/scatter | solution.py:62
  48.2 32.9 %scatter_fusion.1 = bf16[3,192,3584]{2,1,0:T(8,128)(2,1)} fusion(bf16[3,192,3584]{2,1,0:T(8,128)(2,1)} %scatter_fusion, s32[128]{0:T(128)S(1)} %select_bitcast_fusion.1, bf16[128,3584]{1,0:T(8,128)(2,1)} %fusion.11), kind=kCustom, calls=%fused_computation.3 | custom fusion | bytes 2753536 | tf_op jit(solution)/shard_map/scatter | solution.py:63
  81.0 32.4 %scatter_fusion.2 = bf16[3,192,3584]{2,1,0:T(8,128)(2,1)} fusion(bf16[3,192,3584]{2,1,0:T(8,128)(2,1)} %scatter_fusion.1, s32[128]{0:T(128)S(1)} %get-tuple-element.2, bf16[128,3584]{1,0:T(8,128)(2,1)} %fusion.17), kind=kCustom, calls=%fused_computation.4 | custom fusion | bytes 2753536 | tf_op jit(solution)/shard_map/scatter | solution.py:64
  113.5 2.6 copy.20
  116.0 1.6 broadcast_in_dim.8
  117.6 365.5 %all_to_all.10 = bf16[3,8,96,3584]{3,2,0,1:T(8,128)(2,1)S(1)} all-to-all(bf16[3,8,96,3584]{3,2,0,1:T(8,128)(2,1)S(1)} %bitcast.120), channel_id=1, replica_groups=mesh['pipe'=4,'expert'=8] {'expert'}, dimensions={1} | all-to-all | bytes 33030144 | tf_op jit(solution)/shard_map/all_to_all | solution.py:70
  483.1 4.8 fusion.56
  488.0 2.5 fusion.20
  490.4 11.4 %convolution_convert_fusion = bf16[768,3584]{1,0:T(8,128)(2,1)} fusion(bf16[1,3584,256]{2,1,0:T(8,128)(2,1)S(1)} %copy-done, bf16[768,3584]{1,0:T(8,128)(2,1)} %bitcast.124, bf16[1,256,3584]{2,1,0:T(8,128)(2,1)} %param.25, f32[768,256]{1,0:T(8,128)} %fusion.20), kind=kOutput, calls=%fused_computation.7 | convolution fusion | flops 2823094272 | bytes 15466496 | tf_op jit(solution)/shard_map/dot_general | solution.py:31
  501.9 11.8 %convolution_convert_fusion.1 = bf16[768,3584]{1,0:T(8,128)(2,1)} fusion(bf16[1,256,3584]{2,1,0:T(8,128)(2,1)} %param.22, bf16[768,3584]{1,0:T(8,128)(2,1)} %bitcast.123, bf16[1,3584,256]{2,1,0:T(8,128)(2,1)} %param.21), kind=kOutput, calls=%fused_computation.8 | convolution fusion | flops 2822307840 | bytes 14680064 | tf_op jit(solution)/shard_map/dot_general | solution.py:75
  513.7 9.6 %pad_maximum_fusion = bf16[2,8,96,3584]{3,2,0,1:T(8,128)(2,1)} fusion(bf16[1,8,96,3584]{3,2,0,1:T(8,128)(2,1)} %bitcast.121, bf16[1,8,96,3584]{3,2,0,1:T(8,128)(2,1)} %bitcast.122), kind=kLoop, calls=%fused_computation.6 | loop fusion | flops 5505024 | bytes 22020096 | tf_op jit(solution)/shard_map/stack | solution.py:85
  523.2 5.4 all-to-all-start.1
  528.6 238.1 %all-to-all-done.1 = bf16[2,8,96,3584]{3,2,0,1:T(8,128)(2,1)} async-done(((bf16[2,8,96,3584]{3,2,0,1:T(8,128)(2,1)}), bf16[2,8,96,3584]{3,2,0,1:T(8,128)(2,1)}, u32[]{:S(2)}, u32[]{:S(2)}) %all-to-all-start.1) | async-done | bytes 11010080 | tf_op jit(solution)/shard_map/all_to_all | solution.py:88
  766.7 8.7 %convert_reduce_fusion = f32[2,2,96,3584]{3,2,0,1:T(8,128)} fusion(bf16[2,8,96,3584]{3,2,0,1:T(8,128)(2,1)} %all-to-all-done.1), kind=kLoop, calls=%fused_computation.5 | loop fusion | flops 9633792 | bytes 16515072 | tf_op jit(solution)/shard_map/reduce_sum | solution.py:89
  775.4 5.4 fusion.57
  780.9 3.8 gather_fusion.1
  785.1 5.0 gather_fusion
  790.1 3.0 fusion.8
  793.3 22.6 %collective-permute-done = bf16[2,128,3584]{2,1,0:T(8,128)(2,1)S(1)} collective-permute-done((bf16[2,128,3584]{2,1,0:T(8,128)(2,1)S(1)}, bf16[2,128,3584]{2,1,0:T(8,128)(2,1)S(1)}, u32[]{:S(2)}, u32[]{:S(2)}) %collective-permute-start) | collective-permute-done | bytes 1835040 | tf_op jit(solution)/shard_map/ppermute | solution.py:12
  816.0 1.3 fusion.58
  (35 shorter events, 9.3 us)
Async XLA Ops:
  0.6 487.4 %copy-start = (bf16[1,3584,256]{2,1,0:T(8,128)(2,1)S(1)}, bf16[1,3584,256]{2,1,0:T(8,128)(2,1)}, u32[]{:S(2)}) copy-start(bf16[1,3584,256]{2,1,0:T(8,128)(2,1)} %param.24) | copy-start | bytes 5505028
  0.6 9.5 %copy-start.2 = (bf16[1,128,3584]{2,1,0:T(8,128)(2,1)S(1)}, bf16[1,128,3584]{2,1,0:T(8,128)(2,1)}, u32[]{:S(2)}) copy-start(bf16[1,128,3584]{2,1,0:T(8,128)(2,1)} %param.16) | copy-start | bytes 2752516
  8.6 2.8 copy-start.3
  10.2 2.4 copy-start.4
  10.2 2.4 copy-start.6
  523.2 243.5 %all-to-all-start.1 = ((bf16[2,8,96,3584]{3,2,0,1:T(8,128)(2,1)}), bf16[2,8,96,3584]{3,2,0,1:T(8,128)(2,1)}, u32[]{:S(2)}, u32[]{:S(2)}) async-start(bf16[2,8,96,3584]{3,2,0,1:T(8,128)(2,1)} %pad_maximum_fusion), calls=%async_computation.1 | async-start | bytes 22020096 | tf_op jit(solution)/shard_map/all_to_all | solution.py:88
  785.0 5.0 copy-start.5
  793.1 24.2 %copy-start.1 = (bf16[1,3584,256]{2,1,0:T(8,128)(2,1)S(1)}, bf16[1,3584,256]{2,1,0:T(8,128)(2,1)}, u32[]{:S(2)}) copy-start(bf16[1,3584,256]{2,1,0:T(8,128)(2,1)} %param.24) | copy-start | bytes 5505028
  793.3 22.7 %collective-permute-start = (bf16[2,128,3584]{2,1,0:T(8,128)(2,1)S(1)}, bf16[2,128,3584]{2,1,0:T(8,128)(2,1)S(1)}, u32[]{:S(2)}, u32[]{:S(2)}) collective-permute-start(bf16[2,128,3584]{2,1,0:T(8,128)(2,1)S(1)} %pad_maximum_fusion.1), channel_id=1, source_target_pairs={{24,0},{0,8},{8,16},{16,24},{25,1},{1,9},{9,17},{17,25},{26,2},{2,... | collective-permute-start | bytes 5505032 | tf_op jit(solution)/shard_map/ppermute | solution.py:12
where the time goes:
time: 819 us; the launch traced here: 817 us
  blocking collectives  366 us (45%)
  waiting for transfers between devices  261 us (32%)
  local copies, waits for them, and re-layouts  124 us (15%)
  other arithmetic  34.8 us (4%)
  matrix products  25.7 us (3%)
    all_to_all x1, blocking collectives, per_device(): lax.all_to_all(copies, 'expert', split_axis=1, concat_axis=1, tiled=True)  366 us
    all_to_all x1, waiting for transfers between devices, per_device(): lax.all_to_all(result, 'expert', split_axis=1, concat_axis=1, tiled=True)  238 us
    scatter x1, local copies, waits for them, and re-layouts, per_device(): outgoing = outgoing.at[1, where_second].set(normed_second)  32.9 us
    scatter x1, local copies, waits for them, and re-layouts, per_device(): outgoing = outgoing.at[2, where_second].set(scaled_grad)  32.4 us
    scatter x1, local copies, waits for them, and re-layouts, per_device(): outgoing = outgoing.at[0, where_first].set(normed_first)  32.2 us
    ppermute x1, waiting for transfers between devices, shifted(): return lax.ppermute(block, axis, route)  22.6 us
  transfers between devices with their start and end apart: 2, of which 2 were waited for; matrix products, arithmetic and copies ran while one was open for 0% of the time, Pallas kernels for 0%

commit v1 on v0

v1 whole, which is shorter than its diff:
```python
import functools

import jax
import jax.numpy as jnp
from jax import lax
from jax.experimental import pallas as pl
from jax.experimental.pallas import tpu as pltpu
from jax.sharding import PartitionSpec as P

SPLIT = 4
VMEM_LIMIT = 40 * 1024 * 1024
PARAMS = pltpu.CompilerParams(vmem_limit_bytes=VMEM_LIMIT)
WHOLE = pl.BlockSpec(memory_space=pltpu.VMEM)


def shifted(block, axis, distance):
    devices = range(lax.axis_size(axis))
    route = [((i - distance) % len(devices), i) for i in devices]
    return lax.ppermute(block, axis, route)


def swapped(block, bit):
    return lax.ppermute(block, "expert", [(i, i ^ bit) for i in range(lax.axis_size("expert"))])


def to_group(block, distance):
    owners = lax.axis_size("expert")
    return lax.ppermute(
        block, "expert", [(i, (i + distance * SPLIT) % owners) for i in range(owners)]
    )


def width_step(width):
    lanes = width // 128
    return 128 * max(n for n in range(1, 9) if lanes % n == 0)


def dot(left, right, left_dim, right_dim):
    return lax.dot_general(
        left, right, (((left_dim,), (right_dim,)), ((), ())), preferred_element_type=jnp.float32
    )


def slot_numbers(relative):
    tokens = relative.shape[0]
    chosen = relative == lax.broadcasted_iota(jnp.int32, (tokens, 128), 1)
    onehot = jnp.where(chosen, 1.0, 0.0)
    earlier = lax.broadcasted_iota(jnp.int32, (tokens, tokens), 1) < lax.broadcasted_iota(
        jnp.int32, (tokens, tokens), 0
    )
    before = dot(
        jnp.where(earlier, 1.0, 0.0).astype(jnp.bfloat16), onehot.astype(jnp.bfloat16), 1, 0
    )
    return jnp.sum(before * onehot, axis=1, keepdims=True).astype(jnp.int32)


def placement(relative, slots, group, capacity):
    tokens = relative.shape[0]
    columns = lax.broadcasted_iota(jnp.int32, (tokens, capacity), 1)
    inside = jnp.where(relative == group, slots, -1)
    return jnp.where(inside == columns, 1.0, 0.0).astype(jnp.bfloat16)


def inverse_rms_of(acts_ref, step):
    width = acts_ref.shape[1]
    squares = 0.0
    for start in range(0, width, step):
        values = acts_ref[:, start : start + step].astype(jnp.float32)
        squares = squares + jnp.sum(values * values, axis=1, keepdims=True)
    return lax.rsqrt(squares / width + 1e-06)


def prepare_first_body(groups, capacity, step, relative_ref, acts_ref, gain_ref, stay_ref, cross_ref):
    relative = relative_ref[...]
    slots = slot_numbers(relative)
    places = [placement(relative, slots, k, capacity) for k in range(groups)]
    inverse_rms = inverse_rms_of(acts_ref, step)
    for start in range(0, acts_ref.shape[1], step):
        part = slice(start, start + step)
        normed = acts_ref[:, part].astype(jnp.float32) * inverse_rms * gain_ref[:, part]
        normed = normed.astype(jnp.bfloat16)
        stay_ref[:, part] = dot(places[0], normed, 0, 0).astype(jnp.bfloat16)
        for k in range(1, groups):
            cross_ref[k - 1, :, part] = dot(places[k], normed, 0, 0).astype(jnp.bfloat16)


def prepare_second_body(
    groups,
    capacity,
    step,
    relative_ref,
    weight_ref,
    acts_ref,
    grad_ref,
    gain_ref,
    stay_ref,
    cross_ref,
):
    relative = relative_ref[...]
    slots = slot_numbers(relative)
    places = [placement(relative, slots, k, capacity) for k in range(groups)]
    inverse_rms = inverse_rms_of(acts_ref, step)
    for start in range(0, acts_ref.shape[1], step):
        part = slice(start, start + step)
        normed = acts_ref[:, part].astype(jnp.float32) * inverse_rms * gain_ref[:, part]
        scaled = weight_ref[...] * grad_ref[:, part].astype(jnp.float32)
        for row, values in enumerate((normed.astype(jnp.bfloat16), scaled.astype(jnp.bfloat16))):
            stay_ref[row, :, part] = dot(places[0], values, 0, 0).astype(jnp.bfloat16)
            for k in range(1, groups):
                cross_ref[k - 1, row, :, part] = dot(places[k], values, 0, 0).astype(jnp.bfloat16)


def backward_hidden_body(pieces, *refs):
    rows_refs = refs[:pieces]
    up_refs, down_refs = refs[pieces : pieces + 2], refs[pieces + 2 : pieces + 4]
    back_ref, upper_total, hidden_total = refs[pieces + 4 :]
    step, steps = pl.program_id(0), pl.num_programs(0)
    normed = jnp.concatenate([ref[0] for ref in rows_refs], axis=0)
    scaled = jnp.concatenate([ref[1] for ref in rows_refs], axis=0)
    hidden = up_refs[0].shape[1]

    @pl.when(step == 0)
    def _():
        upper_total[...] = jnp.zeros_like(upper_total)
        hidden_total[...] = jnp.zeros_like(hidden_total)

    for lane in range(2):
        part = slice(lane * hidden, (lane + 1) * hidden)
        upper_total[:, part] += dot(normed, up_refs[lane][...], 1, 0)
        hidden_total[:, part] += dot(scaled, down_refs[lane][...], 1, 1)

    @pl.when(step == steps - 1)
    def _():
        upper = upper_total[...]
        sigmoid = jax.nn.sigmoid(upper)
        back = hidden_total[...] * sigmoid * (1.0 + upper * (1.0 - sigmoid))
        back_ref[...] = back.astype(jnp.bfloat16)


def forward_hidden_body(pieces, *refs):
    rows_refs = refs[:pieces]
    up_refs = refs[pieces : pieces + 2]
    hidden_ref, upper_total = refs[pieces + 2 :]
    step, steps = pl.program_id(0), pl.num_programs(0)
    normed = jnp.concatenate([ref[...] for ref in rows_refs], axis=0)
    hidden = up_refs[0].shape[1]

    @pl.when(step == 0)
    def _():
        upper_total[...] = jnp.zeros_like(upper_total)

    for lane in range(2):
        part = slice(lane * hidden, (lane + 1) * hidden)
        upper_total[:, part] += dot(normed, up_refs[lane][...], 1, 0)

    @pl.when(step == steps - 1)
    def _():
        upper = upper_total[...]
        hidden_ref[...] = (upper * jax.nn.sigmoid(upper)).astype(jnp.bfloat16)


def spread_body(weights_dim, own_rows, hidden_ref, one_ref, other_ref, own_ref, away_ref):
    hidden = one_ref.shape[1 - weights_dim] if weights_dim == 0 else one_ref.shape[0]
    hidden = hidden_ref.shape[1] // 2
    contract = 1 if weights_dim == 0 else 0
    total = dot(hidden_ref[:, :hidden], one_ref[...], 1, contract)
    total = total + dot(hidden_ref[:, hidden:], other_ref[...], 1, contract)
    own_ref[...] = total[:own_rows]
    away_ref[...] = total[own_rows:].astype(jnp.bfloat16)


def spread(hidden_rows, one, other, weights_dim, first, length, step):
    own_rows = hidden_rows.shape[0] // 2
    offset = first // step
    if weights_dim == 0:
        block, index = (step, one.shape[1]), lambda j: (j + offset, 0)
    else:
        block, index = (one.shape[0], step), lambda j: (0, j + offset)
    return pl.pallas_call(
        functools.partial(spread_body, weights_dim, own_rows),
        grid=(length // step,),
        in_specs=[
            pl.BlockSpec(hidden_rows.shape, lambda j: (0, 0)),
            pl.BlockSpec(block, index),
            pl.BlockSpec(block, index),
        ],
        out_specs=[pl.BlockSpec((own_rows, step), lambda j: (0, j))] * 2,
        out_shape=[
            jax.ShapeDtypeStruct((own_rows, length), jnp.float32),
            jax.ShapeDtypeStruct((own_rows, length), jnp.bfloat16),
        ],
        compiler_params=PARAMS,
    )(hidden_rows, one, other)


def collected(relative, groups, capacity, own, partner, returned):
    slots = slot_numbers(relative)
    stay = own + partner.astype(jnp.float32)
    high = stay.astype(jnp.bfloat16)
    low = (stay - high.astype(jnp.float32)).astype(jnp.bfloat16)
    here = placement(relative, slots, 0, capacity)
    total = dot(here, high, 1, 0) + dot(here, low, 1, 0)
    away = (groups - 1) * capacity
    columns = lax.broadcasted_iota(jnp.int32, (relative.shape[0], away), 1)
    inside = jnp.where(relative > 0, (relative - 1) * capacity + slots, -1)
    there = jnp.where(inside == columns, 1.0, 0.0).astype(jnp.bfloat16)
    return total + dot(there, returned, 1, 0)


def finish_first_body(
    groups, capacity, relative_ref, weight_ref, acts_ref, own_ref, partner_ref, returned_ref, out_ref
):
    total = collected(
        relative_ref[...], groups, capacity, own_ref[...], partner_ref[...], returned_ref[...]
    )
    out_ref[...] = (acts_ref[...].astype(jnp.float32) + weight_ref[...] * total).astype(
        jnp.bfloat16
    )


def finish_second_body(
    groups,
    capacity,
    step,
    relative_ref,
    acts_ref,
    grad_ref,
    gain_ref,
    own_ref,
    partner_ref,
    returned_ref,
    out_ref,
    gained,
):
    width = acts_ref.shape[1]
    relative = relative_ref[...]
    inverse_rms = inverse_rms_of(acts_ref, step)
    along = 0.0
    for start in range(0, width, step):
        part = slice(start, start + step)
        total = collected(
            relative, groups, capacity, own_ref[:, part], partner_ref[:, part], returned_ref[:, part]
        )
        total = gain_ref[:, part] * total
        gained[:, part] = total
        along = along + jnp.sum(
            acts_ref[:, part].astype(jnp.float32) * total, axis=1, keepdims=True
        )
    scale = inverse_rms * inverse_rms * inverse_rms * (along / width)
    for start in range(0, width, step):
        part = slice(start, start + step)
        values = acts_ref[:, part].astype(jnp.float32)
        out = grad_ref[:, part].astype(jnp.float32) + inverse_rms * gained[:, part] - values * scale
        out_ref[:, part] = out.astype(jnp.bfloat16)


def rows_blocks(arrays, step):
    specs = []
    for array in arrays:
        lead = array.shape[:-1]
        specs.append(pl.BlockSpec((*lead, step), lambda j, zeros=(0,) * len(lead): (*zeros, j)))
    return specs


def per_device(
    acts_first,
    route_first,
    weight_first,
    acts_second,
    grad_second,
    route_second,
    weight_second,
    gain_first,
    up_first,
    down_first,
    gain_second,
    up_second,
    down_second,
):
    owners = lax.axis_size("expert")
    groups = owners // SPLIT
    tokens, width = acts_first.shape[1:]
    capacity = 3 * tokens * SPLIT // (2 * owners)
    away = (groups - 1) * capacity
    step = width_step(width)
    hidden = up_first.shape[2]
    bf16 = jnp.bfloat16
    group = lax.axis_index("expert") // SPLIT
    relative_first = (route_first[0] - group + groups) % groups
    relative_second = (route_second[0] - group + groups) % groups

    down_second_other = swapped(down_second[0], 2)

    stay_second, cross_second = pl.pallas_call(
        functools.partial(prepare_second_body, groups, capacity, step),
        in_specs=[WHOLE] * 5,
        out_specs=[WHOLE] * 2,
        out_shape=[
            jax.ShapeDtypeStruct((2, capacity, width), bf16),
            jax.ShapeDtypeStruct((groups - 1, 2, capacity, width), bf16),
        ],
        compiler_params=PARAMS,
    )(relative_second, weight_second[0], acts_second[0], grad_second[0], gain_second)
    came_second = [to_group(cross_second[k - 1], k) for k in range(1, groups)]
    came_second = came_second[0] if groups == 2 else jnp.concatenate(came_second, axis=1)
    stay_second_other = swapped(stay_second, 1)
    up_second_other = swapped(up_second[0], 2)
    up_first_other = swapped(up_first[0], 1)

    stay_first, cross_first = pl.pallas_call(
        functools.partial(prepare_first_body, groups, capacity, step),
        in_specs=[WHOLE] * 3,
        out_specs=[WHOLE] * 2,
        out_shape=[
            jax.ShapeDtypeStruct((capacity, width), bf16),
            jax.ShapeDtypeStruct((groups - 1, capacity, width), bf16),
        ],
        compiler_params=PARAMS,
    )(relative_first, acts_first[0], gain_first)
    came_first = [to_group(cross_first[k - 1], k) for k in range(1, groups)]
    came_first = came_first[0] if groups == 2 else jnp.concatenate(came_first, axis=0)
    came_second_other = swapped(came_second, 1)
    stay_first_other = swapped(stay_first, 2)
    came_first_other = swapped(came_first, 2)
    down_first_other = swapped(down_first[0], 1)

    rows = [stay_second, came_second, stay_second_other, came_second_other]
    if capacity % 16:
        rows = [jnp.concatenate(rows, axis=1)]
    both = 2 * (capacity + away)
    back_upper = pl.pallas_call(
        functools.partial(backward_hidden_body, len(rows)),
        grid=(width // step,),
        in_specs=rows_blocks(rows, step)
        + [pl.BlockSpec((step, hidden), lambda j: (j, 0))] * 2
        + [pl.BlockSpec((hidden, step), lambda j: (0, j))] * 2,
        out_specs=pl.BlockSpec((both, 2 * hidden), lambda j: (0, 0)),
        out_shape=jax.ShapeDtypeStruct((both, 2 * hidden), bf16),
        scratch_shapes=[pltpu.VMEM((both, 2 * hidden), jnp.float32)] * 2,
        compiler_params=PARAMS,
    )(*rows, up_second[0], up_second_other, down_second[0], down_second_other)
    own_second, send_second = spread(
        back_upper, up_second[0], up_second_other, 0, 0, width, step
    )
    came_part = swapped(send_second[capacity:], 1)
    stay_part = swapped(send_second[:capacity], 1)
    back = (own_second[capacity:] + came_part.astype(jnp.float32)).astype(bf16)
    returned = [
        to_group(back[(k - 1) * capacity : k * capacity], groups - k) for k in range(1, groups)
    ]
    returned = returned[0] if groups == 2 else jnp.concatenate(returned, axis=0)
    grad_acts = pl.pallas_call(
        functools.partial(finish_second_body, groups, capacity, step),
        in_specs=[WHOLE] * 7,
        out_specs=WHOLE,
        out_shape=jax.ShapeDtypeStruct((tokens, width), bf16),
        scratch_shapes=[pltpu.VMEM((tokens, width), jnp.float32)],
        compiler_params=PARAMS,
    )(
        relative_second,
        acts_second[0],
        grad_second[0],
        gain_second,
        own_second[:capacity],
        stay_part,
        returned,
    )
    next_grad = shifted(grad_acts, "pipe", 1)

    rows = [stay_first, came_first, stay_first_other, came_first_other]
    if capacity % 16:
        rows = [jnp.concatenate(rows, axis=0)]
    hidden_first = pl.pallas_call(
        functools.partial(forward_hidden_body, len(rows)),
        grid=(width // step,),
        in_specs=rows_blocks(rows, step) + [pl.BlockSpec((step, hidden), lambda j: (j, 0))] * 2,
        out_specs=pl.BlockSpec((both, 2 * hidden), lambda j: (0, 0)),
        out_shape=jax.ShapeDtypeStruct((both, 2 * hidden), bf16),
        scratch_shapes=[pltpu.VMEM((both, 2 * hidden), jnp.float32)],
        compiler_params=PARAMS,
    )(*rows, up_first[0], up_first_other)
    next_parts = []
    parts = 2 if (width // step) % 2 == 0 else 1
    length = width // parts
    for first in range(0, width, length):
        own_first, send_first = spread(
            hidden_first, down_first[0], down_first_other, 1, first, length, step
        )
        came_part = swapped(send_first[capacity:], 2)
        stay_part = swapped(send_first[:capacity], 2)
        back = (own_first[capacity:] + came_part.astype(jnp.float32)).astype(bf16)
        returned = [
            to_group(back[(k - 1) * capacity : k * capacity], groups - k)
            for k in range(1, groups)
        ]
        returned = returned[0] if groups == 2 else jnp.concatenate(returned, axis=0)
        mixed = pl.pallas_call(
            functools.partial(finish_first_body, groups, capacity),
            in_specs=[WHOLE] * 6,
            out_specs=WHOLE,
            out_shape=jax.ShapeDtypeStruct((tokens, length), bf16),
            compiler_params=PARAMS,
        )(
            relative_first,
            weight_first[0],
            acts_first[0][:, first : first + length],
            own_first[:capacity],
            stay_part,
            returned,
        )
        next_parts.append(shifted(mixed, "pipe", 1))
    next_first = next_parts[0] if parts == 1 else jnp.concatenate(next_parts, axis=1)
    return (next_first[None], next_grad[None])


def solution(mesh):
    in_specs = (
        P("pipe", "expert", None),
        P("pipe", "expert", None),
        P("pipe", "expert", None),
        P("pipe", "expert", None),
        P("pipe", "expert", None),
        P("pipe", "expert", None),
        P("pipe", "expert", None),
        P("pipe", None),
        P("pipe", None, "expert"),
        P("pipe", "expert", None),
        P("pipe", None),
        P("pipe", None, "expert"),
        P("pipe", "expert", None),
    )
    out_specs = (P("pipe", "expert", None), P("pipe", "expert", None))
    return jax.shard_map(
        per_device, mesh=mesh, in_specs=in_specs, out_specs=out_specs, check_vma=False
    )
```

time: 819 us -> 300 us (0.37)
  blocking collectives: 366 us -> 0 us
  local copies, waits for them, and re-layouts: 124 us -> 15.9 us
  waiting for transfers between devices: 261 us -> 227 us
  other arithmetic: 34.8 us -> 2.16 us
  Pallas kernels: 0 us -> 27 us
  matrix products: 25.7 us -> 0 us
  starting transfers between devices: 5.45 us -> 26.3 us
    all_to_all x1 -> x0, blocking collectives: 366 us -> none  [per_device(): lax.all_to_all(copies, 'expert', split_axis=1, concat_axis=1, tiled=True)]
    all_to_all x1 -> x0, waiting for transfers between devices: 238 us -> none  [per_device(): lax.all_to_all(result, 'expert', split_axis=1, concat_axis=1, tiled=True)]
    ppermute x0 -> x19, waiting for transfers between devices: none -> 214 us  [the longest x5 128 us: to_group(): lax.ppermute(block, 'expert', [(i, (i + distance * SPLIT) % owners) for i...]
    scatter x3 -> x0, local copies, waits for them, and re-layouts: 97.5 us -> none  [the longest x1 32.9 us: per_device(): outgoing = outgoing.at[1, where_second].set(normed_second)]
    pallas_call x0 -> x10, Pallas kernels: none -> 27 us  [the longest x3 9.01 us: spread(): pl.pallas_call(functools.partial(spread_body, weights_dim, own_rows), gri...]
    dot_general x3 -> x0, matrix products: 25.7 us -> none  [the longest x1 11.8 us: per_device(): jnp.dot(hidden, down_first[0], preferred_element_type=jnp.float32)]
    ppermute x0 -> x19, starting transfers between devices: none -> 24.5 us  [the longest x14 15 us: swapped(): lax.ppermute(block, 'expert', [(i, i ^ bit) for i in range(lax.axis_size(...]
    reduce_sum x6 -> x0, other arithmetic: 13.8 us -> none  [the longest x1 8.72 us: per_device(): jnp.sum(returned.reshape(2, experts_count, SPLIT, capacity, model_width),...]
  transfers between devices with their start and end apart: 2 -> 22, of which waited for: 2 -> 11; matrix products, arithmetic and copies ran while one was open for 0% -> 1% of each run, Pallas kernels for 0% -> 8%
where the time goes in v1:
time: 300 us; the launch traced here: 299 us
  waiting for transfers between devices  227 us (76%)
  Pallas kernels  27 us (9%)
  starting transfers between devices  26.3 us (9%)
  local copies, waits for them, and re-layouts  15.9 us (5%)
    ppermute x5, waiting for transfers between devices, to_group(): lax.ppermute(block, 'expert', [(i, (i + distance * SPLIT) % owners) for i...  128 us
    ppermute x14, waiting for transfers between devices, swapped(): lax.ppermute(block, 'expert', [(i, i ^ bit) for i in range(lax.axis_size(...  85.8 us
    ppermute x14, starting transfers between devices, swapped(): lax.ppermute(block, 'expert', [(i, i ^ bit) for i in range(lax.axis_size(...  15 us
    ppermute x3, waiting for transfers between devices, shifted(): return lax.ppermute(block, axis, route)  13.4 us
    unnamed x47, local copies, waits for them, and re-layouts  13.3 us
    ppermute x5, starting transfers between devices, to_group(): lax.ppermute(block, 'expert', [(i, (i + distance * SPLIT) % owners) for i...  9.53 us
    pallas_call x3, Pallas kernels, spread(): pl.pallas_call(functools.partial(spread_body, weights_dim, own_rows), gri...  9.01 us
    pallas_call x1, Pallas kernels, per_device(): pl.pallas_call(functools.partial(backward_hidden_body, len(rows)), grid=(...  6.79 us
  transfers between devices with their start and end apart: 22, of which 11 were waited for; matrix products, arithmetic and copies ran while one was open for 1% of the time, Pallas kernels for 8%

profile of v1, /device:TPU:0, one launch (start us, length us, event | category | flops | bytes accessed | tf_op | source)
XLA Modules:
  0.0 299.5 jit_solution(1955299629033897127)
XLA Ops:
  5.4 2.4 shard_map.146
  9.1 4.0 %collective-permute-start.13 = (bf16[2,96,3584]{2,1,0:T(8,128)(2,1)}, bf16[2,96,3584]{2,1,0:T(8,128)(2,1)}, u32[]{:S(2)}, u32[]{:S(2)}) collective-permute-start(bf16[2,96,3584]{2,1,0:T(8,128)(2,1)} %bitcast.11), channel_id=1, source_target_pairs={{0,4},{1,5},{2,6},{3,7},{4,0},{5,1},{6,2},{7,3},{8,12},{9,13},{10,... | collective-permute-start | bytes 4128776 | tf_op jit(solution)/shard_map/ppermute | solution.py:28
  16.8 1.6 collective-permute-start.1
  18.9 83.5 %collective-permute-done.refs_1_ = bf16[96,3584]{1,0:T(8,128)(2,1)S(1)} collective-permute-done((bf16[96,3584]{1,0:T(8,128)(2,1)S(1)}, bf16[96,3584]{1,0:T(8,128)(2,1)S(1)}, u32[]{:S(2)}, u32[]{:S(2)}) %collective-permute-start) | collective-permute-done | bytes 688160 | tf_op jit(solution)/shard_map/ppermute | solution.py:28
  106.9 13.9 %collective-permute-done.2.refs_3_ = bf16[96,3584]{1,0:T(8,128)(2,1)S(1)} collective-permute-done((bf16[96,3584]{1,0:T(8,128)(2,1)S(1)}, bf16[96,3584]{1,0:T(8,128)(2,1)S(1)}, u32[]{:S(2)}, u32[]{:S(2)}) %collective-permute-start.2) | collective-permute-done | bytes 688160 | tf_op jit(solution)/shard_map/ppermute | solution.py:23
  129.9 4.4 %shard_map.141.hidden_ref = bf16[384,512]{1,0:T(8,128)(2,1)S(1)} custom-call(bf16[96,3584]{1,0:T(8,128)(2,1)S(1)} %get-tuple-element.12.refs_0_, bf16[96,3584]{1,0:T(8,128)(2,1)S(1)} %copy-done.12, bf16[96,3584]{1,0:T(8,128)(2,1)S(1)} %copy-done.14, bf16[96,3584]{1,0:T(8,128)(2,1)S(1)} %copy-done.16, bf16[3584,256]{1,0:T(8,128)(2,1)S(1)} %bitcast.33, ...), custom_call_target="tpu_custom_call" | custom-call | tf_op jit(solution)/shard_map/pallas_call | solution.py:373
  134.4 2.4 shard_map.142
  137.5 2.5 shard_map.144
  140.1 15.0 %collective-permute-done.14.refs_2_ = bf16[2,96,3584]{2,1,0:T(8,128)(2,1)} collective-permute-done((bf16[2,96,3584]{2,1,0:T(8,128)(2,1)}, bf16[2,96,3584]{2,1,0:T(8,128)(2,1)}, u32[]{:S(2)}, u32[]{:S(2)}) %collective-permute-start.14) | collective-permute-done | bytes 1376288 | tf_op jit(solution)/shard_map/ppermute | solution.py:23
  155.8 4.5 %collective-permute-done.16.refs_5_.other_ref = bf16[3584,256]{1,0:T(8,128)(2,1)} collective-permute-done((bf16[3584,256]{1,0:T(8,128)(2,1)S(1)}, bf16[3584,256]{1,0:T(8,128)(2,1)}, u32[]{:S(2)}, u32[]{:S(2)}) %collective-permute-start.16) | collective-permute-done | bytes 1835040 | tf_op jit(solution)/shard_map/ppermute | solution.py:23
  160.3 39.3 %collective-permute-done.17.refs_7_ = bf16[256,3584]{1,0:T(8,128)(2,1)} collective-permute-done((bf16[256,3584]{1,0:T(8,128)(2,1)}, bf16[256,3584]{1,0:T(8,128)(2,1)}, u32[]{:S(2)}, u32[]{:S(2)}) %collective-permute-start.17) | collective-permute-done | bytes 1835040 | tf_op jit(solution)/shard_map/ppermute | solution.py:23
  199.6 6.8 %shard_map.147.hidden_ref = bf16[384,512]{1,0:T(8,128)(2,1)S(1)} custom-call(bf16[2,96,3584]{2,1,0:T(8,128)(2,1)S(1)} %copy-done.10, bf16[2,96,3584]{2,1,0:T(8,128)(2,1)} %collective-permute-done.13.refs_1_, bf16[2,96,3584]{2,1,0:T(8,128)(2,1)} %collective-permute-done.14.refs_2_, bf16[2,96,3584]{2,1,0:T(8,128)(2,1)} %collective-permute-done.15.refs_3_, ...), custom_call_target="tpu_custom_call" | custom-call | tf_op jit(solution)/shard_map/pallas_call | solution.py:331
  206.4 4.1 %shard_map.148 = (f32[192,3584]{1,0:T(8,128)S(1)}, bf16[192,3584]{1,0:T(8,128)(2,1)S(1)}) custom-call(bf16[384,512]{1,0:T(8,128)(2,1)S(1)} %shard_map.147.hidden_ref, bf16[3584,256]{1,0:T(8,128)(2,1)S(1)} %bitcast.20, bf16[3584,256]{1,0:T(8,128)(2,1)} %collective-permute-done.16.refs_5_.other_ref), custom_call_target="tpu_custom_call" | custom-call | tf_op jit(solution)/shard_map/pallas_call | solution.py:179
  210.6 1.6 collective-permute-start.19
  214.5 2.1 collective-permute-start.7
  216.6 9.7 %collective-permute-done.19 = bf16[96,3584]{1,0:T(8,128)(2,1)S(1)} collective-permute-done((bf16[96,3584]{1,0:T(8,128)(2,1)S(1)}, bf16[96,3584]{1,0:T(8,128)(2,1)S(1)}, u32[]{:S(2)}, u32[]{:S(2)}) %collective-permute-start.19) | collective-permute-done | bytes 688160 | tf_op jit(solution)/shard_map/ppermute | solution.py:23
  228.0 3.3 %collective-permute-done.10 = bf16[96,1792]{1,0:T(8,128)(2,1)S(1)} collective-permute-done((bf16[96,1792]{1,0:T(8,128)(2,1)S(1)}, bf16[96,1792]{1,0:T(8,128)(2,1)S(1)}, u32[]{:S(2)}, u32[]{:S(2)}) %collective-permute-start.10) | collective-permute-done | bytes 344096 | tf_op jit(solution)/shard_map/ppermute | solution.py:23
  232.0 2.4 collective-permute-start.11
  234.5 1.7 collective-permute-done.7.returned_ref
  237.2 42.7 %collective-permute-done.11.returned_ref = bf16[96,1792]{1,0:T(8,128)(2,1)S(1)} collective-permute-done((bf16[96,1792]{1,0:T(8,128)(2,1)S(1)}, bf16[96,1792]{1,0:T(8,128)(2,1)S(1)}, u32[]{:S(2)}, u32[]{:S(2)}) %collective-permute-start.11) | collective-permute-done | bytes 344096 | tf_op jit(solution)/shard_map/ppermute | solution.py:28
  280.9 1.6 shard_map.149
  282.5 1.7 collective-permute-start.21
  284.2 4.5 %collective-permute-done.12 = bf16[128,1792]{1,0:T(8,128)(2,1)S(1)} collective-permute-done((bf16[128,1792]{1,0:T(8,128)(2,1)S(1)}, bf16[128,1792]{1,0:T(8,128)(2,1)S(1)}, u32[]{:S(2)}, u32[]{:S(2)}) %collective-permute-start.12) | collective-permute-done | bytes 458784 | tf_op jit(solution)/shard_map/ppermute | solution.py:19
  289.7 8.8 %collective-permute-done.21 = bf16[128,3584]{1,0:T(8,128)(2,1)S(1)} collective-permute-done((bf16[128,3584]{1,0:T(8,128)(2,1)S(1)}, bf16[128,3584]{1,0:T(8,128)(2,1)S(1)}, u32[]{:S(2)}, u32[]{:S(2)}) %collective-permute-start.21) | collective-permute-done | bytes 917536 | tf_op jit(solution)/shard_map/ppermute | solution.py:19
  (92 shorter events, 33.7 us)
Async XLA Ops:
  5.4 99.5 %copy-start = (bf16[1,3584,256]{2,1,0:T(8,128)(2,1)S(1)}, bf16[1,3584,256]{2,1,0:T(8,128)(2,1)}, u32[]{:S(2)}) copy-start(bf16[1,3584,256]{2,1,0:T(8,128)(2,1)} %param.24) | copy-start | bytes 5505028
  9.1 97.1 %collective-permute-start.13 = (bf16[2,96,3584]{2,1,0:T(8,128)(2,1)}, bf16[2,96,3584]{2,1,0:T(8,128)(2,1)}, u32[]{:S(2)}, u32[]{:S(2)}) collective-permute-start(bf16[2,96,3584]{2,1,0:T(8,128)(2,1)} %bitcast.11), channel_id=1, source_target_pairs={{0,4},{1,5},{2,6},{3,7},{4,0},{5,1},{6,2},{7,3},{8,12},{9,13},{10,... | collective-permute-start | bytes 4128776 | tf_op jit(solution)/shard_map/ppermute | solution.py:28
  13.1 110.2 %collective-permute-start.3 = (bf16[3584,256]{1,0:T(8,128)(2,1)}, bf16[3584,256]{1,0:T(8,128)(2,1)}, u32[]{:S(2)}, u32[]{:S(2)}) collective-permute-start(bf16[3584,256]{1,0:T(8,128)(2,1)} %bitcast.32), channel_id=1, source_target_pairs={{0,1},{1,0},{2,3},{3,2},{4,5},{5,4},{6,7},{7,6},{8,9},{9,8},{10,11... | collective-permute-start | bytes 5505032 | tf_op jit(solution)/shard_map/ppermute | solution.py:23
  16.4 86.1 %collective-permute-start = (bf16[96,3584]{1,0:T(8,128)(2,1)S(1)}, bf16[96,3584]{1,0:T(8,128)(2,1)S(1)}, u32[]{:S(2)}, u32[]{:S(2)}) collective-permute-start(bf16[96,3584]{1,0:T(8,128)(2,1)S(1)} %bitcast.34), channel_id=1, source_target_pairs={{0,4},{1,5},{2,6},{3,7},{4,0},{5,1},{6,2},{7,3},{8,12},{9,13},{10,... | collective-permute-start | bytes 2064392 | tf_op jit(solution)/shard_map/ppermute | solution.py:28
  16.8 87.2 %collective-permute-start.1 = (bf16[96,3584]{1,0:T(8,128)(2,1)S(1)}, bf16[96,3584]{1,0:T(8,128)(2,1)S(1)}, u32[]{:S(2)}, u32[]{:S(2)}) collective-permute-start(bf16[96,3584]{1,0:T(8,128)(2,1)S(1)} %get-tuple-element.12.refs_0_), channel_id=1, source_target_pairs={{0,2},{1,3},{2,0},{3,1},{4,6},{5,7},{6,4},{7,5},{8,10},{9,11},{10,... | collective-permute-start | bytes 2064392 | tf_op jit(solution)/shard_map/ppermute | solution.py:23
  18.4 116.0 %collective-permute-start.4 = (bf16[256,3584]{1,0:T(8,128)(2,1)}, bf16[256,3584]{1,0:T(8,128)(2,1)}, u32[]{:S(2)}, u32[]{:S(2)}) collective-permute-start(bf16[256,3584]{1,0:T(8,128)(2,1)} %bitcast.21), channel_id=1, source_target_pairs={{0,1},{1,0},{2,3},{3,2},{4,5},{5,4},{6,7},{7,6},{8,9},{9,8},{10,11... | collective-permute-start | bytes 5505032 | tf_op jit(solution)/shard_map/ppermute | solution.py:23
  102.5 18.4 %collective-permute-start.2 = (bf16[96,3584]{1,0:T(8,128)(2,1)S(1)}, bf16[96,3584]{1,0:T(8,128)(2,1)S(1)}, u32[]{:S(2)}, u32[]{:S(2)}) collective-permute-start(bf16[96,3584]{1,0:T(8,128)(2,1)S(1)} %collective-permute-done.refs_1_), channel_id=1, source_target_pairs={{0,2},{1,3},{2,0},{3,1},{4,6},{5,7},{6,4},{7,5},{8,10},{9,11},{10,... | collective-permute-start | bytes 2064392 | tf_op jit(solution)/shard_map/ppermute | solution.py:23
  104.9 55.4 %collective-permute-start.16 = (bf16[3584,256]{1,0:T(8,128)(2,1)S(1)}, bf16[3584,256]{1,0:T(8,128)(2,1)}, u32[]{:S(2)}, u32[]{:S(2)}) collective-permute-start(bf16[3584,256]{1,0:T(8,128)(2,1)S(1)} %bitcast.18), channel_id=1, source_target_pairs={{0,2},{1,3},{2,0},{3,1},{4,6},{5,7},{6,4},{7,5},{8,10},{9,11},{10,... | collective-permute-start | bytes 5505032 | tf_op jit(solution)/shard_map/ppermute | solution.py:23
  106.2 93.4 %collective-permute-start.17 = (bf16[256,3584]{1,0:T(8,128)(2,1)}, bf16[256,3584]{1,0:T(8,128)(2,1)}, u32[]{:S(2)}, u32[]{:S(2)}) collective-permute-start(bf16[256,3584]{1,0:T(8,128)(2,1)} %bitcast.30), channel_id=1, source_target_pairs={{0,2},{1,3},{2,0},{3,1},{4,6},{5,7},{6,4},{7,5},{8,10},{9,11},{10,... | collective-permute-start | bytes 5505032 | tf_op jit(solution)/shard_map/ppermute | solution.py:23
  121.7 33.4 %collective-permute-start.14 = (bf16[2,96,3584]{2,1,0:T(8,128)(2,1)}, bf16[2,96,3584]{2,1,0:T(8,128)(2,1)}, u32[]{:S(2)}, u32[]{:S(2)}) collective-permute-start(bf16[2,96,3584]{2,1,0:T(8,128)(2,1)} %copy-done.9), channel_id=1, source_target_pairs={{0,1},{1,0},{2,3},{3,2},{4,5},{5,4},{6,7},{7,6},{8,9},{9,8},{10,11... | collective-permute-start | bytes 4128776 | tf_op jit(solution)/shard_map/ppermute | solution.py:23
  123.3 76.3 %collective-permute-start.15 = (bf16[2,96,3584]{2,1,0:T(8,128)(2,1)}, bf16[2,96,3584]{2,1,0:T(8,128)(2,1)}, u32[]{:S(2)}, u32[]{:S(2)}) collective-permute-start(bf16[2,96,3584]{2,1,0:T(8,128)(2,1)} %collective-permute-done.13.refs_1_), channel_id=1, source_target_pairs={{0,1},{1,0},{2,3},{3,2},{4,5},{5,4},{6,7},{7,6},{8,9},{9,8},{10,11... | collective-permute-start | bytes 4128776 | tf_op jit(solution)/shard_map/ppermute | solution.py:23
  136.8 62.8 %copy-start.7 = (bf16[1,256,3584]{2,1,0:T(8,128)(2,1)S(1)}, bf16[1,256,3584]{2,1,0:T(8,128)(2,1)}, u32[]{:S(2)}) copy-start(bf16[1,256,3584]{2,1,0:T(8,128)(2,1)} %param.25) | copy-start | bytes 5505028
  136.8 77.5 %collective-permute-start.6 = (bf16[96,1792]{1,0:T(8,128)(2,1)S(1)}, bf16[96,1792]{1,0:T(8,128)(2,1)S(1)}, u32[]{:S(2)}, u32[]{:S(2)}) collective-permute-start(bf16[96,1792]{1,0:T(8,128)(2,1)S(1)} %get-tuple-element.32), channel_id=1, source_target_pairs={{0,2},{1,3},{2,0},{3,1},{4,6},{5,7},{6,4},{7,5},{8,10},{9,11},{10,... | collective-permute-start | bytes 1032200 | tf_op jit(solution)/shard_map/ppermute | solution.py:23
  155.1 76.8 %collective-permute-start.5 = (bf16[96,1792]{1,0:T(8,128)(2,1)S(1)}, bf16[96,1792]{1,0:T(8,128)(2,1)S(1)}, u32[]{:S(2)}, u32[]{:S(2)}) collective-permute-start(bf16[96,1792]{1,0:T(8,128)(2,1)S(1)} %get-tuple-element.33), channel_id=1, source_target_pairs={{0,2},{1,3},{2,0},{3,1},{4,6},{5,7},{6,4},{7,5},{8,10},{9,11},{10,... | collective-permute-start | bytes 1032200 | tf_op jit(solution)/shard_map/ppermute | solution.py:23
  210.6 15.7 %collective-permute-start.19 = (bf16[96,3584]{1,0:T(8,128)(2,1)S(1)}, bf16[96,3584]{1,0:T(8,128)(2,1)S(1)}, u32[]{:S(2)}, u32[]{:S(2)}) collective-permute-start(bf16[96,3584]{1,0:T(8,128)(2,1)S(1)} %get-tuple-element.24), channel_id=1, source_target_pairs={{0,1},{1,0},{2,3},{3,2},{4,5},{5,4},{6,7},{7,6},{8,9},{9,8},{10,11... | collective-permute-start | bytes 2064392 | tf_op jit(solution)/shard_map/ppermute | solution.py:23
  212.3 19.1 %collective-permute-start.10 = (bf16[96,1792]{1,0:T(8,128)(2,1)S(1)}, bf16[96,1792]{1,0:T(8,128)(2,1)S(1)}, u32[]{:S(2)}, u32[]{:S(2)}) collective-permute-start(bf16[96,1792]{1,0:T(8,128)(2,1)S(1)} %get-tuple-element.34), channel_id=1, source_target_pairs={{0,2},{1,3},{2,0},{3,1},{4,6},{5,7},{6,4},{7,5},{8,10},{9,11},{10,... | collective-permute-start | bytes 1032200 | tf_op jit(solution)/shard_map/ppermute | solution.py:23
  212.9 24.3 %collective-permute-start.9 = (bf16[96,1792]{1,0:T(8,128)(2,1)S(1)}, bf16[96,1792]{1,0:T(8,128)(2,1)S(1)}, u32[]{:S(2)}, u32[]{:S(2)}) collective-permute-start(bf16[96,1792]{1,0:T(8,128)(2,1)S(1)} %get-tuple-element.35), channel_id=1, source_target_pairs={{0,2},{1,3},{2,0},{3,1},{4,6},{5,7},{6,4},{7,5},{8,10},{9,11},{10,... | collective-permute-start | bytes 1032200 | tf_op jit(solution)/shard_map/ppermute | solution.py:23
  214.5 21.8 %collective-permute-start.7 = (bf16[96,1792]{1,0:T(8,128)(2,1)S(1)}, bf16[96,1792]{1,0:T(8,128)(2,1)S(1)}, u32[]{:S(2)}, u32[]{:S(2)}) collective-permute-start(bf16[96,1792]{1,0:T(8,128)(2,1)S(1)} %get-tuple-element.26), channel_id=1, source_target_pairs={{0,4},{1,5},{2,6},{3,7},{4,0},{5,1},{6,2},{7,3},{8,12},{9,13},{10,... | collective-permute-start | bytes 1032200 | tf_op jit(solution)/shard_map/ppermute | solution.py:28
  226.3 54.6 %collective-permute-start.18 = (bf16[96,3584]{1,0:T(8,128)(2,1)S(1)}, bf16[96,3584]{1,0:T(8,128)(2,1)S(1)}, u32[]{:S(2)}, u32[]{:S(2)}) collective-permute-start(bf16[96,3584]{1,0:T(8,128)(2,1)S(1)} %get-tuple-element.25), channel_id=1, source_target_pairs={{0,1},{1,0},{2,3},{3,2},{4,5},{5,4},{6,7},{7,6},{8,9},{9,8},{10,11... | collective-permute-start | bytes 2064392 | tf_op jit(solution)/shard_map/ppermute | solution.py:23
  231.3 49.5 %collective-permute-start.20 = (bf16[96,3584]{1,0:T(8,128)(2,1)S(1)}, bf16[96,3584]{1,0:T(8,128)(2,1)S(1)}, u32[]{:S(2)}, u32[]{:S(2)}) collective-permute-start(bf16[96,3584]{1,0:T(8,128)(2,1)S(1)} %get-tuple-element.22), channel_id=1, source_target_pairs={{0,4},{1,5},{2,6},{3,7},{4,0},{5,1},{6,2},{7,3},{8,12},{9,13},{10,... | collective-permute-start | bytes 2064392 | tf_op jit(solution)/shard_map/ppermute | solution.py:28
  232.0 47.9 %collective-permute-start.11 = (bf16[96,1792]{1,0:T(8,128)(2,1)S(1)}, bf16[96,1792]{1,0:T(8,128)(2,1)S(1)}, u32[]{:S(2)}, u32[]{:S(2)}) collective-permute-start(bf16[96,1792]{1,0:T(8,128)(2,1)S(1)} %get-tuple-element.28), channel_id=1, source_target_pairs={{0,4},{1,5},{2,6},{3,7},{4,0},{5,1},{6,2},{7,3},{8,12},{9,13},{10,... | collective-permute-start | bytes 1032200 | tf_op jit(solution)/shard_map/ppermute | solution.py:28
  237.1 47.0 %collective-permute-start.8 = (bf16[128,1792]{1,0:T(8,128)(2,1)S(1)}, bf16[128,1792]{1,0:T(8,128)(2,1)S(1)}, u32[]{:S(2)}, u32[]{:S(2)}) collective-permute-start(bf16[128,1792]{1,0:T(8,128)(2,1)S(1)} %shard_map.143), channel_id=1, source_target_pairs={{24,0},{0,8},{8,16},{16,24},{25,1},{1,9},{9,17},{17,25},{26,2},{2,... | collective-permute-start | bytes 1376264 | tf_op jit(solution)/shard_map/ppermute | solution.py:19
  280.8 8.0 %collective-permute-start.12 = (bf16[128,1792]{1,0:T(8,128)(2,1)S(1)}, bf16[128,1792]{1,0:T(8,128)(2,1)S(1)}, u32[]{:S(2)}, u32[]{:S(2)}) collective-permute-start(bf16[128,1792]{1,0:T(8,128)(2,1)S(1)} %shard_map.145), channel_id=1, source_target_pairs={{24,0},{0,8},{8,16},{16,24},{25,1},{1,9},{9,17},{17,25},{26,2},{2,... | collective-permute-start | bytes 1376264 | tf_op jit(solution)/shard_map/ppermute | solution.py:19
  282.5 16.0 %collective-permute-start.21 = (bf16[128,3584]{1,0:T(8,128)(2,1)S(1)}, bf16[128,3584]{1,0:T(8,128)(2,1)S(1)}, u32[]{:S(2)}, u32[]{:S(2)}) collective-permute-start(bf16[128,3584]{1,0:T(8,128)(2,1)S(1)} %shard_map.149), channel_id=1, source_target_pairs={{24,0},{0,8},{8,16},{16,24},{25,1},{1,9},{9,17},{17,25},{26,2},{2,... | collective-permute-start | bytes 2752520 | tf_op jit(solution)/shard_map/ppermute | solution.py:19
  (21 other events, 286.0 us)

commit v2 on v1

--- a/solution.py
+++ b/solution.py
@@ -9,6 +9,7 @@
 
 SPLIT = 4
 VMEM_LIMIT = 40 * 1024 * 1024
+PREPARE_LIMIT = 60 * 1024 * 1024
 PARAMS = pltpu.CompilerParams(vmem_limit_bytes=VMEM_LIMIT)
 WHOLE = pl.BlockSpec(memory_space=pltpu.VMEM)
 
@@ -23,6 +24,10 @@
     return lax.ppermute(block, "expert", [(i, i ^ bit) for i in range(lax.axis_size("expert"))])
 
 
+def after(block, *others):
+    return lax.optimization_barrier((block, *others))[0]
+
+
 def to_group(block, distance):
     owners = lax.axis_size("expert")
     return lax.ppermute(
@@ -39,6 +44,20 @@
     return lax.dot_general(
         left, right, (((left_dim,), (right_dim,)), ((), ())), preferred_element_type=jnp.float32
     )
+
+
+def as_column(row):
+    tokens = row.shape[1]
+    diagonal = lax.broadcasted_iota(jnp.int32, (tokens, tokens), 0) == lax.broadcasted_iota(
+        jnp.int32, (tokens, tokens), 1
+    )
+    return jnp.sum(jnp.where(diagonal, row, 0.0), axis=1, keepdims=True)
+
+
+def relative_groups(route_ref, groups):
+    group = lax.axis_index("expert") // SPLIT
+    ahead = as_column(route_ref[...].astype(jnp.float32)).astype(jnp.int32) - group
+    return jnp.where(ahead < 0, ahead + groups, ahead)
 
 
 def slot_numbers(relative):
@@ -70,44 +89,88 @@
     return lax.rsqrt(squares / width + 1e-06)
 
 
-def prepare_first_body(groups, capacity, step, relative_ref, acts_ref, gain_ref, stay_ref, cross_ref):
-    relative = relative_ref[...]
-    slots = slot_numbers(relative)
-    places = [placement(relative, slots, k, capacity) for k in range(groups)]
-    inverse_rms = inverse_rms_of(acts_ref, step)
-    for start in range(0, acts_ref.shape[1], step):
-        part = slice(start, start + step)
-        normed = acts_ref[:, part].astype(jnp.float32) * inverse_rms * gain_ref[:, part]
-        normed = normed.astype(jnp.bfloat16)
-        stay_ref[:, part] = dot(places[0], normed, 0, 0).astype(jnp.bfloat16)
-        for k in range(1, groups):
-            cross_ref[k - 1, :, part] = dot(places[k], normed, 0, 0).astype(jnp.bfloat16)
-
-
-def prepare_second_body(
+def prepare_body(
     groups,
     capacity,
     step,
-    relative_ref,
+    route_first_ref,
+    route_second_ref,
     weight_ref,
-    acts_ref,
+    acts_first_hbm,
+    gain_first_hbm,
+    acts_second_hbm,
+    gain_second_hbm,
+    grad_hbm,
+    stay_first_ref,
+    stay_second_ref,
+    cross_first_ref,
+    cross_second_ref,
+    acts_first_ref,
+    gain_first_ref,
+    acts_second_ref,
+    gain_second_ref,
     grad_ref,
-    gain_ref,
-    stay_ref,
-    cross_ref,
+    sems,
 ):
-    relative = relative_ref[...]
-    slots = slot_numbers(relative)
-    places = [placement(relative, slots, k, capacity) for k in range(groups)]
-    inverse_rms = inverse_rms_of(acts_ref, step)
-    for start in range(0, acts_ref.shape[1], step):
-        part = slice(start, start + step)
-        normed = acts_ref[:, part].astype(jnp.float32) * inverse_rms * gain_ref[:, part]
-        scaled = weight_ref[...] * grad_ref[:, part].astype(jnp.float32)
-        for row, values in enumerate((normed.astype(jnp.bfloat16), scaled.astype(jnp.bfloat16))):
-            stay_ref[row, :, part] = dot(places[0], values, 0, 0).astype(jnp.bfloat16)
-            for k in range(1, groups):
-                cross_ref[k - 1, row, :, part] = dot(places[k], values, 0, 0).astype(jnp.bfloat16)
+    sources = (acts_second_hbm, gain_second_hbm, grad_hbm, acts_first_hbm, gain_first_hbm)
+    targets = (acts_second_ref, gain_second_ref, grad_ref, acts_first_ref, gain_first_ref)
+    copies = [
+        pltpu.make_async_copy(source, target, sems.at[n])
+        for n, (source, target) in enumerate(zip(sources, targets))
+    ]
+    for copy in copies:
+        copy.start()
+    weight = as_column(weight_ref[...])
+    places = []
+    for route_ref in (route_first_ref, route_second_ref):
+        relative = relative_groups(route_ref, groups)
+        slots = slot_numbers(relative)
+        places.append([placement(relative, slots, k, capacity) for k in range(groups)])
+
+    def place(batch, row, stay_ref, cross_ref, value, part):
+        stay_ref[row, :, part] = dot(places[batch][0], value, 0, 0).astype(jnp.bfloat16)
+        for k in range(1, groups):
+            there = dot(places[batch][k], value, 0, 0).astype(jnp.bfloat16)
+            cross_ref[k - 1, row, :, part] = there
+
+    parts = [
+        slice(start, start + step) for start in range(0, acts_first_ref.shape[1], step)
+    ]
+    for copy in copies[:2]:
+        copy.wait()
+    inverse_rms = inverse_rms_of(acts_second_ref, step)
+    for part in parts:
+        normed = acts_second_ref[:, part].astype(jnp.float32) * inverse_rms * gain_second_ref[:, part]
+        place(1, 0, stay_second_ref, cross_second_ref, normed.astype(jnp.bfloat16), part)
+    copies[2].wait()
+    for part in parts:
+        scaled = weight * grad_ref[:, part].astype(jnp.float32)
+        place(1, 1, stay_second_ref, cross_second_ref, scaled.astype(jnp.bfloat16), part)
+    for copy in copies[3:]:
+        copy.wait()
+    inverse_rms = inverse_rms_of(acts_first_ref, step)
+    for part in parts:
+        normed = acts_first_ref[:, part].astype(jnp.float32) * inverse_rms * gain_first_ref[:, part]
+        place(0, 0, stay_first_ref, cross_first_ref, normed.astype(jnp.bfloat16), part)
+
+
+def prepare(groups, capacity, step, route_first, route_second, weight, *large):
+    width = large[0].shape[1]
+    shape = jax.ShapeDtypeStruct
+    return pl.pallas_call(
+        functools.partial(prepare_body, groups, capacity, step),
+        in_specs=[WHOLE] * 3 + [pl.BlockSpec(memory_space=pl.ANY)] * 5,
+        out_specs=[WHOLE] * 4,
+        out_shape=[
+            shape((1, capacity, width), jnp.bfloat16),
+            shape((2, capacity, width), jnp.bfloat16),
+            shape((groups - 1, 1, capacity, width), jnp.bfloat16),
+            shape((groups - 1, 2, capacity, width), jnp.bfloat16),
+        ],
+        scratch_shapes=[pltpu.VMEM(array.shape, array.dtype) for array in large]
+        + [pltpu.SemaphoreType.DMA((5,))],
+        compiler_params=pltpu.CompilerParams(vmem_limit_bytes=PREPARE_LIMIT),
+    )(route_first, route_second, weight, *large)
 
 
 def backward_hidden_body(pieces, *refs):
@@ -142,7 +205,7 @@
     up_refs = refs[pieces : pieces + 2]
     hidden_ref, upper_total = refs[pieces + 2 :]
     step, steps = pl.program_id(0), pl.num_programs(0)
-    normed = jnp.concatenate([ref[...] for ref in rows_refs], axis=0)
+    normed = jnp.concatenate([ref[0] for ref in rows_refs], axis=0)
     hidden = up_refs[0].shape[1]
 
     @pl.when(step == 0)
@@ -160,7 +223,6 @@
 
 
 def spread_body(weights_dim, own_rows, hidden_ref, one_ref, other_ref, own_ref, away_ref):
-    hidden = one_ref.shape[1 - weights_dim] if weights_dim == 0 else one_ref.shape[0]
     hidden = hidden_ref.shape[1] // 2
     contract = 1 if weights_dim == 0 else 0
     total = dot(hidden_ref[:, :hidden], one_ref[...], 1, contract)
@@ -208,21 +270,19 @@
 
 
 def finish_first_body(
-    groups, capacity, relative_ref, weight_ref, acts_ref, own_ref, partner_ref, returned_ref, out_ref
+    groups, capacity, route_ref, weight_ref, acts_ref, own_ref, partner_ref, returned_ref, out_ref
 ):
-    total = collected(
-        relative_ref[...], groups, capacity, own_ref[...], partner_ref[...], returned_ref[...]
-    )
-    out_ref[...] = (acts_ref[...].astype(jnp.float32) + weight_ref[...] * total).astype(
-        jnp.bfloat16
-    )
+    relative = relative_groups(route_ref, groups)
+    total = collected(relative, groups, capacity, own_ref[...], partner_ref[...], returned_ref[...])
+    weight = as_column(weight_ref[...])
+    out_ref[...] = (acts_ref[...].astype(jnp.float32) + weight * total).astype(jnp.bfloat16)
 
 
 def finish_second_body(
     groups,
     capacity,
     step,
-    relative_ref,
+    route_ref,
     acts_ref,
     grad_ref,
     gain_ref,
@@ -233,7 +293,7 @@
     gained,
 ):
     width = acts_ref.shape[1]
-    relative = relative_ref[...]
+    relative = relative_groups(route_ref, groups)
     inverse_rms = inverse_rms_of(acts_ref, step)
     along = 0.0
     for start in range(0, width, step):
@@ -252,6 +312,10 @@
         values = acts_ref[:, part].astype(jnp.float32)
         out = grad_ref[:, part].astype(jnp.float32) + inverse_rms * gained[:, part] - values * scale
         out_ref[:, part] = out.astype(jnp.bfloat16)
+
+
+def columns_block(length, number, rows):
+    return pl.BlockSpec((rows, length), lambda j: (0, number))
 
 
 def rows_blocks(arrays, step):
@@ -285,44 +349,40 @@
     step = width_step(width)
     hidden = up_first.shape[2]
     bf16 = jnp.bfloat16
-    group = lax.axis_index("expert") // SPLIT
-    relative_first = (route_first[0] - group + groups) % groups
-    relative_second = (route_second[0] - group + groups) % groups
+    routes = [route.reshape(1, tokens) for route in (route_first, route_second)]
+    weights = [weight.reshape(1, tokens) for weight in (weight_first, weight_second)]
+    parts = 2 if (width // step) % 2 == 0 else 1
+    length = width // parts
+    starts = range(0, width, length)
 
     down_second_other = swapped(down_second[0], 2)
-
-    stay_second, cross_second = pl.pallas_call(
-        functools.partial(prepare_second_body, groups, capacity, step),
-        in_specs=[WHOLE] * 5,
-        out_specs=[WHOLE] * 2,
-        out_shape=[
-            jax.ShapeDtypeStruct((2, capacity, width), bf16),
-            jax.ShapeDtypeStruct((groups - 1, 2, capacity, width), bf16),
-        ],
-        compiler_params=PARAMS,
-    )(relative_second, weight_second[0], acts_second[0], grad_second[0], gain_second)
-    came_second = [to_group(cross_second[k - 1], k) for k in range(1, groups)]
-    came_second = came_second[0] if groups == 2 else jnp.concatenate(came_second, axis=1)
-    stay_second_other = swapped(stay_second, 1)
-    up_second_other = swapped(up_second[0], 2)
     up_first_other = swapped(up_first[0], 1)
-
-    stay_first, cross_first = pl.pallas_call(
-        functools.partial(prepare_first_body, groups, capacity, step),
-        in_specs=[WHOLE] * 3,
-        out_specs=[WHOLE] * 2,
-        out_shape=[
-            jax.ShapeDtypeStruct((capacity, width), bf16),
-            jax.ShapeDtypeStruct((groups - 1, capacity, width), bf16),
-        ],
-        compiler_params=PARAMS,
-    )(relative_first, acts_first[0], gain_first)
-    came_first = [to_group(cross_first[k - 1], k) for k in range(1, groups)]
-    came_first = came_first[0] if groups == 2 else jnp.concatenate(came_first, axis=0)
+    stay_first, stay_second, cross_first, cross_second = prepare(
+        groups,
+        capacity,
+        step,
+        *routes,
+        weights[1],
+        acts_first[0],
+        gain_first,
+        acts_second[0],
+        gain_second,
+        grad_second[0],
+    )
+
+    def crossed(blocks):
+        came = [to_group(blocks[k - 1], k) for k in range(1, groups)]
+        return came[0] if groups == 2 else jnp.concatenate(came, axis=1)
+
+    came_second = crossed(cross_second)
+    stay_second_other = swapped(after(stay_second, up_first_other), 1)
+    up_second_other = swapped(after(up_second[0], up_first_other), 2)
+    came_first = crossed(after(cross_first, up_second_other))
+    down_first_other = swapped(after(down_first[0], up_first_other), 1)
+    came_second = after(came_second, down_second_other, stay_second_other)
     came_second_other = swapped(came_second, 1)
-    stay_first_other = swapped(stay_first, 2)
+    stay_first_other = swapped(after(stay_first, up_second_other), 2)
     came_first_other = swapped(came_first, 2)
-    down_first_other = swapped(down_first[0], 1)
 
     rows = [stay_second, came_second, stay_second_other, came_second_other]
     if capacity % 16:
@@ -344,11 +404,41 @@
     )
     came_part = swapped(send_second[capacity:], 1)
     stay_part = swapped(send_second[:capacity], 1)
-    back = (own_second[capacity:] + came_part.astype(jnp.float32)).astype(bf16)
+    def first_hidden(rows):
+        if capacity % 16:
+            rows = [jnp.concatenate(rows, axis=1)]
+        count = sum(array.shape[1] for array in rows)
+        return pl.pallas_call(
+            functools.partial(forward_hidden_body, len(rows)),
+            grid=(width // step,),
+            in_specs=rows_blocks(rows, step) + [pl.BlockSpec((step, hidden), lambda j: (j, 0))] * 2,
+            out_specs=pl.BlockSpec((count, 2 * hidden), lambda j: (0, 0)),
+            out_shape=jax.ShapeDtypeStruct((count, 2 * hidden), bf16),
+            scratch_shapes=[pltpu.VMEM((count, 2 * hidden), jnp.float32)],
+            compiler_params=PARAMS,
+        )(*rows, up_first[0], up_first_other)
+
+    weights_down = (down_first[0], down_first_other, 1)
+    stay_hidden = first_hidden([after(stay_first, send_second), stay_first_other])
+    stay_own, stay_send = spread(stay_hidden, *weights_down, 0, width, step)
+    stay_first_part = swapped(stay_send, 2)
+    back = (own_second[capacity:] + after(came_part, stay_send).astype(jnp.float32)).astype(bf16)
     returned = [
         to_group(back[(k - 1) * capacity : k * capacity], groups - k) for k in range(1, groups)
     ]
     returned = returned[0] if groups == 2 else jnp.concatenate(returned, axis=0)
+    came_hidden = first_hidden([came_first, after(came_first_other, stay_send)])
+    spreads = [spread(came_hidden, *weights_down, first, length, step) for first in starts]
+    came_parts = [swapped(send, 2) for _, send in spreads]
+    returned_first = []
+    for (own, _), part in zip(spreads, came_parts):
+        back = (own + part.astype(jnp.float32)).astype(bf16)
+        blocks = [
+            to_group(back[(k - 1) * capacity : k * capacity], groups - k)
+            for k in range(1, groups)
+        ]
+        returned_first.append(blocks[0] if groups == 2 else jnp.concatenate(blocks, axis=0))
+
     grad_acts = pl.pallas_call(
         functools.partial(finish_second_body, groups, capacity, step),
         in_specs=[WHOLE] * 7,
@@ -357,7 +447,7 @@
         scratch_shapes=[pltpu.VMEM((tokens, width), jnp.float32)],
         compiler_params=PARAMS,
     )(
-        relative_second,
+        routes[1],
         acts_second[0],
         grad_second[0],
         gain_second,
@@ -366,47 +456,24 @@
         returned,
     )
     next_grad = shifted(grad_acts, "pipe", 1)
-
-    rows = [stay_first, came_first, stay_first_other, came_first_other]
-    if capacity % 16:
-        rows = [jnp.concatenate(rows, axis=0)]
-    hidden_first = pl.pallas_call(
-        functools.partial(forward_hidden_body, len(rows)),
-        grid=(width // step,),
-        in_specs=rows_blocks(rows, step) + [pl.BlockSpec((step, hidden), lambda j: (j, 0))] * 2,
-        out_specs=pl.BlockSpec((both, 2 * hidden), lambda j: (0, 0)),
-        out_shape=jax.ShapeDtypeStruct((both, 2 * hidden), bf16),
-        scratch_shapes=[pltpu.VMEM((both, 2 * hidden), jnp.float32)],
-        compiler_params=PARAMS,
-    )(*rows, up_first[0], up_first_other)
     next_parts = []
-    parts = 2 if (width // step) % 2 == 0 else 1
-    length = width // parts
-    for first in range(0, width, length):
-        own_first, send_first = spread(
-            hidden_first, down_first[0], down_first_other, 1, first, length, step
-        )
-        came_part = swapped(send_first[capacity:], 2)
-        stay_part = swapped(send_first[:capacity], 2)
-        back = (own_first[capacity:] + came_part.astype(jnp.float32)).astype(bf16)
-        returned = [
-            to_group(back[(k - 1) * capacity : k * capacity], groups - k)
-            for k in range(1, groups)
-        ]
-        returned = returned[0] if groups == 2 else jnp.concatenate(returned, axis=0)
+    order = [grad_acts, next_grad]
+    for first, back in zip(starts, returned_first):
+        half = functools.partial(columns_block, length, first // length)
         mixed = pl.pallas_call(
             functools.partial(finish_first_body, groups, capacity),
-            in_specs=[WHOLE] * 6,
+            grid=(1,),
+            in_specs=[WHOLE] * 2 + [half(tokens), half(capacity), half(capacity), WHOLE],
             out_specs=WHOLE,
             out_shape=jax.ShapeDtypeStruct((tokens, length), bf16),
             compiler_params=PARAMS,
         )(
-            relative_first,
-            weight_first[0],
-            acts_first[0][:, first : first + length],
-            own_first[:capacity],
-            stay_part,
-            returned,
+            routes[0],
+            weights[0],
+            after(acts_first[0], order[first > 0]),
+            stay_own,
+            stay_first_part,
+            back,
         )
         next_parts.append(shifted(mixed, "pipe", 1))
     next_first = next_parts[0] if parts == 1 else jnp.concatenate(next_parts, axis=1)

time: 300 us -> 239 us (0.80)
  waiting for transfers between devices: 227 us -> 179 us
  local copies, waits for them, and re-layouts: 15.9 us -> 5.42 us
    ppermute x5, waiting for transfers between devices: 128 us -> 69.6 us  [to_group(): lax.ppermute(block, 'expert', [(i, (i + distance * SPLIT) % owners) for i...]
    ppermute x14 -> x13, waiting for transfers between devices: 85.8 us -> 101 us  [swapped(): lax.ppermute(block, 'expert', [(i, i ^ bit) for i in range(lax.axis_size(...]
    unnamed x47 -> x29, local copies, waits for them, and re-layouts: 13.3 us -> 5.32 us
    ppermute x3, waiting for transfers between devices: 13.4 us -> 7.89 us  [shifted(): return lax.ppermute(block, axis, route)]
    pallas_call x3 -> x4, Pallas kernels: 9.01 us -> 6.83 us  [spread(): pl.pallas_call(functools.partial(spread_body, weights_dim, own_rows), gri...]
    ppermute x14 -> x13, starting transfers between devices: 15 us -> 16.9 us  [swapped(): lax.ppermute(block, 'expert', [(i, i ^ bit) for i in range(lax.axis_size(...]
  transfers between devices with their start and end apart: 22 -> 21, of which waited for: 11 -> 11; matrix products, arithmetic and copies ran while one was open for 1% -> 0% of each run, Pallas kernels for 8% -> 11%
where the time goes in v2:
time: 239 us
  waiting for transfers between devices  179 us (75%)
  starting transfers between devices  27.6 us (12%)
  Pallas kernels  25.2 us (11%)
  local copies, waits for them, and re-layouts  5.42 us (2%)
    ppermute x13, waiting for transfers between devices, swapped(): lax.ppermute(block, 'expert', [(i, i ^ bit) for i in range(lax.axis_size(...  101 us
    ppermute x5, waiting for transfers between devices, to_group(): lax.ppermute(block, 'expert', [(i, (i + distance * SPLIT) % owners) for i...  69.6 us
    ppermute x13, starting transfers between devices, swapped(): lax.ppermute(block, 'expert', [(i, i ^ bit) for i in range(lax.axis_size(...  16.9 us
    ppermute x5, starting transfers between devices, to_group(): lax.ppermute(block, 'expert', [(i, (i + distance * SPLIT) % owners) for i...  10.5 us
    ppermute x3, waiting for transfers between devices, shifted(): return lax.ppermute(block, axis, route)  7.89 us
    pallas_call x4, Pallas kernels, spread(): pl.pallas_call(functools.partial(spread_body, weights_dim, own_rows), gri...  6.83 us
    pallas_call x1, Pallas kernels, per_device(): pl.pallas_call(functools.partial(backward_hidden_body, len(rows)), grid=(...  6.29 us
    unnamed x29, local copies, waits for them, and re-layouts  5.32 us
  transfers between devices with their start and end apart: 21, of which 11 were waited for; matrix products, arithmetic and copies ran while one was open for 0% of the time, Pallas kernels for 11%

profile of v2, /device:TPU:0, one launch (start us, length us, event | category | flops | bytes accessed | tf_op | source)
XLA Modules:
  0.0 239.2 jit_solution(3790417879447903055)
XLA Ops:
  0.6 3.0 %collective-permute-start.2 = (bf16[3584,256]{1,0:T(8,128)(2,1)}, bf16[3584,256]{1,0:T(8,128)(2,1)S(1)}, u32[]{:S(2)}, u32[]{:S(2)}) collective-permute-start(bf16[3584,256]{1,0:T(8,128)(2,1)} %bitcast.23), channel_id=1, source_target_pairs={{0,1},{1,0},{2,3},{3,2},{4,5},{5,4},{6,7},{7,6},{8,9},{9,8},{10,11... | collective-permute-start | bytes 5505032 | tf_op jit(solution)/shard_map/ppermute | solution.py:24
  3.6 1.6 collective-permute-start.1
  5.2 5.2 %shard_map.140 = (bf16[1,96,3584]{2,1,0:T(8,128)(2,1)}, bf16[2,96,3584]{2,1,0:T(8,128)(2,1)}, bf16[1,1,96,3584]{3,2,1,0:T(8,128)(2,1)}, bf16[1,2,96,3584]{3,2,1,0:T(8,128)(2,1)}) custom-call(s32[1,128]{1,0:T(1,128)} %bitcast.35, s32[1,128]{1,0:T(1,128)} %bitcast.40, f32[1,128]{1,0:T(1,128)} %bitcast.43, bf16[128,3584]{1,0:T(8,128)(2,1)} %bitcast.20, ...), custom_call_target="tpu_custom_call" | custom-call | tf_op jit(solution)/shard_map/pallas_call | solution.py:160
  10.5 2.7 %collective-permute-start = (bf16[2,96,3584]{2,1,0:T(8,128)(2,1)}, bf16[2,96,3584]{2,1,0:T(8,128)(2,1)S(1)}, u32[]{:S(2)}, u32[]{:S(2)}) collective-permute-start(bf16[2,96,3584]{2,1,0:T(8,128)(2,1)} %bitcast.44), channel_id=1, source_target_pairs={{0,4},{1,5},{2,6},{3,7},{4,0},{5,1},{6,2},{7,3},{8,12},{9,13},{10,... | collective-permute-start | bytes 4128776 | tf_op jit(solution)/shard_map/ppermute | solution.py:33
  13.1 30.8 %collective-permute-done.2.refs_3_ = bf16[3584,256]{1,0:T(8,128)(2,1)S(1)} collective-permute-done((bf16[3584,256]{1,0:T(8,128)(2,1)}, bf16[3584,256]{1,0:T(8,128)(2,1)S(1)}, u32[]{:S(2)}, u32[]{:S(2)}) %collective-permute-start.2) | collective-permute-done | bytes 1835040 | tf_op jit(solution)/shard_map/ppermute | solution.py:24
  43.9 1.7 collective-permute-start.3
  47.2 28.3 %collective-permute-done.refs_1_ = bf16[2,96,3584]{2,1,0:T(8,128)(2,1)S(1)} collective-permute-done((bf16[2,96,3584]{2,1,0:T(8,128)(2,1)}, bf16[2,96,3584]{2,1,0:T(8,128)(2,1)S(1)}, u32[]{:S(2)}, u32[]{:S(2)}) %collective-permute-start) | collective-permute-done | bytes 1376288 | tf_op jit(solution)/shard_map/ppermute | solution.py:33
  78.4 35.7 %collective-permute-done.5.refs_5_.other_ref = bf16[3584,256]{1,0:T(8,128)(2,1)S(1)} collective-permute-done((bf16[3584,256]{1,0:T(8,128)(2,1)}, bf16[3584,256]{1,0:T(8,128)(2,1)S(1)}, u32[]{:S(2)}, u32[]{:S(2)}) %collective-permute-start.5) | collective-permute-done | bytes 1835040 | tf_op jit(solution)/shard_map/ppermute | solution.py:24
  115.7 2.6 %collective-permute-start.12 = (bf16[1,96,3584]{2,1,0:T(8,128)(2,1)}, bf16[1,96,3584]{2,1,0:T(8,128)(2,1)S(1)}, u32[]{:S(2)}, u32[]{:S(2)}) collective-permute-start(bf16[1,96,3584]{2,1,0:T(8,128)(2,1)} %bitcast.45), channel_id=1, source_target_pairs={{0,4},{1,5},{2,6},{3,7},{4,0},{5,1},{6,2},{7,3},{8,12},{9,13},{10,... | collective-permute-start | bytes 2064392 | tf_op jit(solution)/shard_map/ppermute | solution.py:33
  122.7 6.3 %shard_map.141.hidden_ref = bf16[384,512]{1,0:T(8,128)(2,1)S(1)} custom-call(bf16[2,96,3584]{2,1,0:T(8,128)(2,1)S(1)} %copy-done.8, bf16[2,96,3584]{2,1,0:T(8,128)(2,1)S(1)} %collective-permute-done.refs_1_, bf16[2,96,3584]{2,1,0:T(8,128)(2,1)S(1)} %collective-permute-done.3.refs_2_, bf16[2,96,3584]{2,1,0:T(8,128)(2,1)S(1)} %collective-permute-done.4.refs_3_, ...), custom_call_target="tpu_custom_call" | custom-call | tf_op jit(solution)/shard_map/pallas_call | solution.py:391
  129.0 2.7 %shard_map.142 = (f32[192,3584]{1,0:T(8,128)S(1)}, bf16[192,3584]{1,0:T(8,128)(2,1)S(1)}) custom-call(bf16[384,512]{1,0:T(8,128)(2,1)S(1)} %shard_map.141.hidden_ref, bf16[3584,256]{1,0:T(8,128)(2,1)S(1)} %bitcast.28, bf16[3584,256]{1,0:T(8,128)(2,1)S(1)} %collective-permute-done.5.refs_5_.other_ref), custom_call_target="tpu_custom_call" | custom-call | tf_op jit(solution)/shard_map/pallas_call | solution.py:241
  132.4 15.0 %collective-permute-done.12.refs_0_ = bf16[1,96,3584]{2,1,0:T(8,128)(2,1)S(1)} collective-permute-done((bf16[1,96,3584]{2,1,0:T(8,128)(2,1)}, bf16[1,96,3584]{2,1,0:T(8,128)(2,1)S(1)}, u32[]{:S(2)}, u32[]{:S(2)}) %collective-permute-start.12) | collective-permute-done | bytes 688160 | tf_op jit(solution)/shard_map/ppermute | solution.py:33
  148.3 1.9 shard_map.143.hidden_ref
  150.2 2.0 shard_map.144
  152.3 11.3 %collective-permute-done.7 = bf16[96,3584]{1,0:T(8,128)(2,1)S(1)} collective-permute-done((bf16[96,3584]{1,0:T(8,128)(2,1)S(1)}, bf16[96,3584]{1,0:T(8,128)(2,1)S(1)}, u32[]{:S(2)}, u32[]{:S(2)}) %collective-permute-start.7) | collective-permute-done | bytes 688160 | tf_op jit(solution)/shard_map/ppermute | solution.py:24
  163.8 2.4 %collective-permute-start.10 = (bf16[96,3584]{1,0:T(8,128)(2,1)S(1)}, bf16[96,3584]{1,0:T(8,128)(2,1)S(1)}, u32[]{:S(2)}, u32[]{:S(2)}) collective-permute-start(bf16[96,3584]{1,0:T(8,128)(2,1)S(1)} %get-tuple-element.48), channel_id=1, source_target_pairs={{0,4},{1,5},{2,6},{3,7},{4,0},{5,1},{6,2},{7,3},{8,12},{9,13},{10,... | collective-permute-start | bytes 2064392 | tf_op jit(solution)/shard_map/ppermute | solution.py:33
  166.2 1.9 shard_map.146.hidden_ref
  169.2 1.9 collective-permute-start.14
  172.3 1.9 collective-permute-start.18
  175.0 15.4 %collective-permute-done.10.returned_ref = bf16[96,3584]{1,0:T(8,128)(2,1)S(1)} collective-permute-done((bf16[96,3584]{1,0:T(8,128)(2,1)S(1)}, bf16[96,3584]{1,0:T(8,128)(2,1)S(1)}, u32[]{:S(2)}, u32[]{:S(2)}) %collective-permute-start.10) | collective-permute-done | bytes 688160 | tf_op jit(solution)/shard_map/ppermute | solution.py:33
  193.2 21.6 %collective-permute-done.18 = bf16[96,1792]{1,0:T(8,128)(2,1)S(1)} collective-permute-done((bf16[96,1792]{1,0:T(8,128)(2,1)S(1)}, bf16[96,1792]{1,0:T(8,128)(2,1)S(1)}, u32[]{:S(2)}, u32[]{:S(2)}) %collective-permute-start.18) | collective-permute-done | bytes 344096 | tf_op jit(solution)/shard_map/ppermute | solution.py:24
  214.9 1.8 collective-permute-start.19
  217.6 10.9 %collective-permute-done.19.returned_ref = bf16[96,1792]{1,0:T(8,128)(2,1)S(1)} collective-permute-done((bf16[96,1792]{1,0:T(8,128)(2,1)S(1)}, bf16[96,1792]{1,0:T(8,128)(2,1)S(1)}, u32[]{:S(2)}, u32[]{:S(2)}) %collective-permute-start.19) | collective-permute-done | bytes 344096 | tf_op jit(solution)/shard_map/ppermute | solution.py:33
  229.4 7.9 %collective-permute-done.20 = bf16[128,1792]{1,0:T(8,128)(2,1)S(1)} collective-permute-done((bf16[128,1792]{1,0:T(8,128)(2,1)S(1)}, bf16[128,1792]{1,0:T(8,128)(2,1)S(1)}, u32[]{:S(2)}, u32[]{:S(2)}) %collective-permute-start.20) | collective-permute-done | bytes 458784 | tf_op jit(solution)/shard_map/ppermute | solution.py:20
  (63 shorter events, 21.9 us)
Async XLA Ops:
  0.6 76.3 %copy-start = (bf16[1,256,3584]{2,1,0:T(8,128)(2,1)S(1)}, bf16[1,256,3584]{2,1,0:T(8,128)(2,1)}, u32[]{:S(2)}) copy-start(bf16[1,256,3584]{2,1,0:T(8,128)(2,1)} %param.22) | copy-start | bytes 5505028
  0.6 43.2 %collective-permute-start.2 = (bf16[3584,256]{1,0:T(8,128)(2,1)}, bf16[3584,256]{1,0:T(8,128)(2,1)S(1)}, u32[]{:S(2)}, u32[]{:S(2)}) collective-permute-start(bf16[3584,256]{1,0:T(8,128)(2,1)} %bitcast.23), channel_id=1, source_target_pairs={{0,1},{1,0},{2,3},{3,2},{4,5},{5,4},{6,7},{7,6},{8,9},{9,8},{10,11... | collective-permute-start | bytes 5505032 | tf_op jit(solution)/shard_map/ppermute | solution.py:24
  3.6 72.7 %collective-permute-start.1 = (bf16[256,3584]{1,0:T(8,128)(2,1)}, bf16[256,3584]{1,0:T(8,128)(2,1)}, u32[]{:S(2)}, u32[]{:S(2)}) collective-permute-start(bf16[256,3584]{1,0:T(8,128)(2,1)} %bitcast.33), channel_id=1, source_target_pairs={{0,2},{1,3},{2,0},{3,1},{4,6},{5,7},{6,4},{7,5},{8,10},{9,11},{10,... | collective-permute-start | bytes 5505032 | tf_op jit(solution)/shard_map/ppermute | solution.py:24
  10.5 65.0 %collective-permute-start = (bf16[2,96,3584]{2,1,0:T(8,128)(2,1)}, bf16[2,96,3584]{2,1,0:T(8,128)(2,1)S(1)}, u32[]{:S(2)}, u32[]{:S(2)}) collective-permute-start(bf16[2,96,3584]{2,1,0:T(8,128)(2,1)} %bitcast.44), channel_id=1, source_target_pairs={{0,4},{1,5},{2,6},{3,7},{4,0},{5,1},{6,2},{7,3},{8,12},{9,13},{10,... | collective-permute-start | bytes 4128776 | tf_op jit(solution)/shard_map/ppermute | solution.py:33
  43.9 32.5 %collective-permute-start.3 = (bf16[2,96,3584]{2,1,0:T(8,128)(2,1)}, bf16[2,96,3584]{2,1,0:T(8,128)(2,1)S(1)}, u32[]{:S(2)}, u32[]{:S(2)}) collective-permute-start(bf16[2,96,3584]{2,1,0:T(8,128)(2,1)} %get-tuple-element.27.refs_0_), channel_id=1, source_target_pairs={{0,1},{1,0},{2,3},{3,2},{4,5},{5,4},{6,7},{7,6},{8,9},{9,8},{10,11... | collective-permute-start | bytes 4128776 | tf_op jit(solution)/shard_map/ppermute | solution.py:24
  45.6 68.5 %collective-permute-start.5 = (bf16[3584,256]{1,0:T(8,128)(2,1)}, bf16[3584,256]{1,0:T(8,128)(2,1)S(1)}, u32[]{:S(2)}, u32[]{:S(2)}) collective-permute-start(bf16[3584,256]{1,0:T(8,128)(2,1)} %bitcast.26), channel_id=1, source_target_pairs={{0,2},{1,3},{2,0},{3,1},{4,6},{5,7},{6,4},{7,5},{8,10},{9,11},{10,... | collective-permute-start | bytes 5505032 | tf_op jit(solution)/shard_map/ppermute | solution.py:24
  76.4 41.9 %collective-permute-start.4 = (bf16[2,96,3584]{2,1,0:T(8,128)(2,1)S(1)}, bf16[2,96,3584]{2,1,0:T(8,128)(2,1)S(1)}, u32[]{:S(2)}, u32[]{:S(2)}) collective-permute-start(bf16[2,96,3584]{2,1,0:T(8,128)(2,1)S(1)} %collective-permute-done.refs_1_), channel_id=1, source_target_pairs={{0,1},{1,0},{2,3},{3,2},{4,5},{5,4},{6,7},{7,6},{8,9},{9,8},{10,11... | collective-permute-start | bytes 4128776 | tf_op jit(solution)/shard_map/ppermute | solution.py:24
  77.0 73.2 %collective-permute-start.9 = (bf16[256,3584]{1,0:T(8,128)(2,1)S(1)}, bf16[256,3584]{1,0:T(8,128)(2,1)S(1)}, u32[]{:S(2)}, u32[]{:S(2)}) collective-permute-start(bf16[256,3584]{1,0:T(8,128)(2,1)S(1)} %bitcast.16), channel_id=1, source_target_pairs={{0,1},{1,0},{2,3},{3,2},{4,5},{5,4},{6,7},{7,6},{8,9},{9,8},{10,11... | collective-permute-start | bytes 5505032 | tf_op jit(solution)/shard_map/ppermute | solution.py:24
  114.1 34.2 %collective-permute-start.8 = (bf16[1,96,3584]{2,1,0:T(8,128)(2,1)}, bf16[1,96,3584]{2,1,0:T(8,128)(2,1)S(1)}, u32[]{:S(2)}, u32[]{:S(2)}) collective-permute-start(bf16[1,96,3584]{2,1,0:T(8,128)(2,1)} %get-tuple-element.34.refs_0_), channel_id=1, source_target_pairs={{0,2},{1,3},{2,0},{3,1},{4,6},{5,7},{6,4},{7,5},{8,10},{9,11},{10,... | collective-permute-start | bytes 2064392 | tf_op jit(solution)/shard_map/ppermute | solution.py:24
  115.7 31.7 %collective-permute-start.12 = (bf16[1,96,3584]{2,1,0:T(8,128)(2,1)}, bf16[1,96,3584]{2,1,0:T(8,128)(2,1)S(1)}, u32[]{:S(2)}, u32[]{:S(2)}) collective-permute-start(bf16[1,96,3584]{2,1,0:T(8,128)(2,1)} %bitcast.45), channel_id=1, source_target_pairs={{0,4},{1,5},{2,6},{3,7},{4,0},{5,1},{6,2},{7,3},{8,12},{9,13},{10,... | collective-permute-start | bytes 2064392 | tf_op jit(solution)/shard_map/ppermute | solution.py:33
  131.8 31.8 %collective-permute-start.7 = (bf16[96,3584]{1,0:T(8,128)(2,1)S(1)}, bf16[96,3584]{1,0:T(8,128)(2,1)S(1)}, u32[]{:S(2)}, u32[]{:S(2)}) collective-permute-start(bf16[96,3584]{1,0:T(8,128)(2,1)S(1)} %get-tuple-element.50), channel_id=1, source_target_pairs={{0,1},{1,0},{2,3},{3,2},{4,5},{5,4},{6,7},{7,6},{8,9},{9,8},{10,11... | collective-permute-start | bytes 2064392 | tf_op jit(solution)/shard_map/ppermute | solution.py:24
  147.4 18.8 %collective-permute-start.13 = (bf16[1,96,3584]{2,1,0:T(8,128)(2,1)S(1)}, bf16[1,96,3584]{2,1,0:T(8,128)(2,1)S(1)}, u32[]{:S(2)}, u32[]{:S(2)}) collective-permute-start(bf16[1,96,3584]{2,1,0:T(8,128)(2,1)S(1)} %collective-permute-done.12.refs_0_), channel_id=1, source_target_pairs={{0,2},{1,3},{2,0},{3,1},{4,6},{5,7},{6,4},{7,5},{8,10},{9,11},{10,... | collective-permute-start | bytes 2064392 | tf_op jit(solution)/shard_map/ppermute | solution.py:24
  147.8 27.2 %collective-permute-start.6 = (bf16[96,3584]{1,0:T(8,128)(2,1)S(1)}, bf16[96,3584]{1,0:T(8,128)(2,1)S(1)}, u32[]{:S(2)}, u32[]{:S(2)}) collective-permute-start(bf16[96,3584]{1,0:T(8,128)(2,1)S(1)} %get-tuple-element.51), channel_id=1, source_target_pairs={{0,1},{1,0},{2,3},{3,2},{4,5},{5,4},{6,7},{7,6},{8,9},{9,8},{10,11... | collective-permute-start | bytes 2064392 | tf_op jit(solution)/shard_map/ppermute | solution.py:24
  163.8 26.6 %collective-permute-start.10 = (bf16[96,3584]{1,0:T(8,128)(2,1)S(1)}, bf16[96,3584]{1,0:T(8,128)(2,1)S(1)}, u32[]{:S(2)}, u32[]{:S(2)}) collective-permute-start(bf16[96,3584]{1,0:T(8,128)(2,1)S(1)} %get-tuple-element.48), channel_id=1, source_target_pairs={{0,4},{1,5},{2,6},{3,7},{4,0},{5,1},{6,2},{7,3},{8,12},{9,13},{10,... | collective-permute-start | bytes 2064392 | tf_op jit(solution)/shard_map/ppermute | solution.py:33
  169.2 22.9 %collective-permute-start.14 = (bf16[96,1792]{1,0:T(8,128)(2,1)S(1)}, bf16[96,1792]{1,0:T(8,128)(2,1)S(1)}, u32[]{:S(2)}, u32[]{:S(2)}) collective-permute-start(bf16[96,1792]{1,0:T(8,128)(2,1)S(1)} %get-tuple-element.44), channel_id=1, source_target_pairs={{0,2},{1,3},{2,0},{3,1},{4,6},{5,7},{6,4},{7,5},{8,10},{9,11},{10,... | collective-permute-start | bytes 1032200 | tf_op jit(solution)/shard_map/ppermute | solution.py:24
  171.0 45.7 %collective-permute-start.11 = (bf16[96,3584]{1,0:T(8,128)(2,1)S(1)}, bf16[96,3584]{1,0:T(8,128)(2,1)S(1)}, u32[]{:S(2)}, u32[]{:S(2)}) collective-permute-start(bf16[96,3584]{1,0:T(8,128)(2,1)S(1)} %get-tuple-element.36), channel_id=1, source_target_pairs={{0,2},{1,3},{2,0},{3,1},{4,6},{5,7},{6,4},{7,5},{8,10},{9,11},{10,... | collective-permute-start | bytes 2064392 | tf_op jit(solution)/shard_map/ppermute | solution.py:24
  172.3 42.5 %collective-permute-start.18 = (bf16[96,1792]{1,0:T(8,128)(2,1)S(1)}, bf16[96,1792]{1,0:T(8,128)(2,1)S(1)}, u32[]{:S(2)}, u32[]{:S(2)}) collective-permute-start(bf16[96,1792]{1,0:T(8,128)(2,1)S(1)} %get-tuple-element.47), channel_id=1, source_target_pairs={{0,2},{1,3},{2,0},{3,1},{4,6},{5,7},{6,4},{7,5},{8,10},{9,11},{10,... | collective-permute-start | bytes 1032200 | tf_op jit(solution)/shard_map/ppermute | solution.py:24
  192.0 24.7 %copy-start.1 = (bf16[1,128,3584]{2,1,0:T(8,128)(2,1)S(1)}, bf16[1,128,3584]{2,1,0:T(8,128)(2,1)}, u32[]{:S(2)}) copy-start(bf16[1,128,3584]{2,1,0:T(8,128)(2,1)} %param.13) | copy-start | bytes 2752516
  192.0 24.7 %copy-start.11 = (s32[1,128,1]{1,2,0:T(1,128)S(1)}, s32[1,128,1]{1,2,0:T(1,128)}, u32[]{:S(2)}) copy-start(s32[1,128,1]{1,2,0:T(1,128)} %param.14) | copy-start | bytes 1540
  192.0 25.6 %collective-permute-start.17 = (bf16[128,3584]{1,0:T(8,128)(2,1)S(1)}, bf16[128,3584]{1,0:T(8,128)(2,1)S(1)}, u32[]{:S(2)}, u32[]{:S(2)}) collective-permute-start(bf16[128,3584]{1,0:T(8,128)(2,1)S(1)} %shard_map.145), channel_id=1, source_target_pairs={{24,0},{0,8},{8,16},{16,24},{25,1},{1,9},{9,17},{17,25},{26,2},{2,... | collective-permute-start | bytes 2752520 | tf_op jit(solution)/shard_map/ppermute | solution.py:20
  192.2 24.5 %collective-permute-start.15 = (bf16[96,1792]{1,0:T(8,128)(2,1)S(1)}, bf16[96,1792]{1,0:T(8,128)(2,1)S(1)}, u32[]{:S(2)}, u32[]{:S(2)}) collective-permute-start(bf16[96,1792]{1,0:T(8,128)(2,1)S(1)} %add_convert_fusion.2), channel_id=1, source_target_pairs={{0,4},{1,5},{2,6},{3,7},{4,0},{5,1},{6,2},{7,3},{8,12},{9,13},{10,... | collective-permute-start | bytes 1032200 | tf_op jit(solution)/shard_map/ppermute | solution.py:33
  214.9 13.6 %collective-permute-start.19 = (bf16[96,1792]{1,0:T(8,128)(2,1)S(1)}, bf16[96,1792]{1,0:T(8,128)(2,1)S(1)}, u32[]{:S(2)}, u32[]{:S(2)}) collective-permute-start(bf16[96,1792]{1,0:T(8,128)(2,1)S(1)} %add_convert_fusion.1), channel_id=1, source_target_pairs={{0,4},{1,5},{2,6},{3,7},{4,0},{5,1},{6,2},{7,3},{8,12},{9,13},{10,... | collective-permute-start | bytes 1032200 | tf_op jit(solution)/shard_map/ppermute | solution.py:33
  217.5 11.9 %collective-permute-start.16 = (bf16[128,1792]{1,0:T(8,128)(2,1)S(1)}, bf16[128,1792]{1,0:T(8,128)(2,1)S(1)}, u32[]{:S(2)}, u32[]{:S(2)}) collective-permute-start(bf16[128,1792]{1,0:T(8,128)(2,1)S(1)} %shard_map.148), channel_id=1, source_target_pairs={{24,0},{0,8},{8,16},{16,24},{25,1},{1,9},{9,17},{17,25},{26,2},{2,... | collective-permute-start | bytes 1376264 | tf_op jit(solution)/shard_map/ppermute | solution.py:20
  229.3 8.0 %collective-permute-start.20 = (bf16[128,1792]{1,0:T(8,128)(2,1)S(1)}, bf16[128,1792]{1,0:T(8,128)(2,1)S(1)}, u32[]{:S(2)}, u32[]{:S(2)}) collective-permute-start(bf16[128,1792]{1,0:T(8,128)(2,1)S(1)} %shard_map.150), channel_id=1, source_target_pairs={{24,0},{0,8},{8,16},{16,24},{25,1},{1,9},{9,17},{17,25},{26,2},{2,... | collective-permute-start | bytes 1376264 | tf_op jit(solution)/shard_map/ppermute | solution.py:20
  (11 other events, 153.6 us)

commit v3 on v2

--- a/solution.py
+++ b/solution.py
@@ -12,6 +12,16 @@
 PREPARE_LIMIT = 60 * 1024 * 1024
 PARAMS = pltpu.CompilerParams(vmem_limit_bytes=VMEM_LIMIT)
 WHOLE = pl.BlockSpec(memory_space=pltpu.VMEM)
+
+
+def to_group_ahead(block, distance):
+    owners, stages = lax.axis_size("expert"), lax.axis_size("pipe")
+    route = [
+        (p * owners + i, (p + 1) % stages * owners + (i + distance * SPLIT) % owners)
+        for p in range(stages)
+        for i in range(owners)
+    ]
+    return lax.ppermute(block, ("pipe", "expert"), route)
 
 
 def shifted(block, axis, distance):
@@ -255,6 +265,13 @@
     )(hidden_rows, one, other)
 
 
+def away_placement(relative, groups, capacity):
+    away = (groups - 1) * capacity
+    columns = lax.broadcasted_iota(jnp.int32, (relative.shape[0], away), 1)
+    inside = jnp.where(relative > 0, (relative - 1) * capacity + slot_numbers(relative), -1)
+    return jnp.where(inside == columns, 1.0, 0.0).astype(jnp.bfloat16)
+
+
 def collected(relative, groups, capacity, own, partner, returned):
     slots = slot_numbers(relative)
     stay = own + partner.astype(jnp.float32)
@@ -262,20 +279,41 @@
     low = (stay - high.astype(jnp.float32)).astype(jnp.bfloat16)
     here = placement(relative, slots, 0, capacity)
     total = dot(here, high, 1, 0) + dot(here, low, 1, 0)
-    away = (groups - 1) * capacity
-    columns = lax.broadcasted_iota(jnp.int32, (relative.shape[0], away), 1)
-    inside = jnp.where(relative > 0, (relative - 1) * capacity + slots, -1)
-    there = jnp.where(inside == columns, 1.0, 0.0).astype(jnp.bfloat16)
-    return total + dot(there, returned, 1, 0)
-
-
-def finish_first_body(
-    groups, capacity, route_ref, weight_ref, acts_ref, own_ref, partner_ref, returned_ref, out_ref
+    return total + dot(away_placement(relative, groups, capacity), returned, 1, 0)
+
+
+def finish_stay_body(
+    groups, capacity, step, route_ref, weight_ref, acts_ref, own_ref, partner_ref, *out_refs
 ):
     relative = relative_groups(route_ref, groups)
-    total = collected(relative, groups, capacity, own_ref[...], partner_ref[...], returned_ref[...])
+    here = placement(relative, slot_numbers(relative), 0, capacity)
     weight = as_column(weight_ref[...])
-    out_ref[...] = (acts_ref[...].astype(jnp.float32) + weight * total).astype(jnp.bfloat16)
+    for start in range(0, acts_ref.shape[1], step):
+        part = slice(start, start + step)
+        stay = own_ref[:, part] + partner_ref[:, part].astype(jnp.float32)
+        high = stay.astype(jnp.bfloat16)
+        low = (stay - high.astype(jnp.float32)).astype(jnp.bfloat16)
+        total = dot(here, high, 1, 0) + dot(here, low, 1, 0)
+        out = acts_ref[:, part].astype(jnp.float32) + weight * total
+        length = out_refs[0].shape[1]
+        first = start % length
+        out_refs[start // length][:, first : first + step] = out.astype(jnp.bfloat16)
+
+
+def finish_came_body(groups, capacity, part, pieces, notes_ref, returned_ref, *refs):
+    out_hbm, out_ref, sem = refs[-3:]
+    relative = relative_groups(notes_ref.at[0:1], groups)
+    there = away_placement(relative, groups, capacity)
+    weight = as_column(notes_ref[1:2])
+    width = out_ref.shape[1] // pieces
+    for n, stayed_ref in enumerate(refs[:pieces]):
+        piece = slice(n * width, (n + 1) * width)
+        total = dot(there, returned_ref[:, piece], 1, 0)
+        out = stayed_ref[...].astype(jnp.float32) + weight * total
+        out_ref[:, piece] = out.astype(jnp.bfloat16)
+    copy = pltpu.make_async_copy(out_ref, out_hbm.at[:, part], sem)
+    copy.start()
+    copy.wait()
 
 
 def finish_second_body(
@@ -314,10 +352,6 @@
         out_ref[:, part] = out.astype(jnp.bfloat16)
 
 
-def columns_block(length, number, rows):
-    return pl.BlockSpec((rows, length), lambda j: (0, number))
-
-
 def rows_blocks(arrays, step):
     specs = []
     for array in arrays:
@@ -351,9 +385,22 @@
     bf16 = jnp.bfloat16
     routes = [route.reshape(1, tokens) for route in (route_first, route_second)]
     weights = [weight.reshape(1, tokens) for weight in (weight_first, weight_second)]
-    parts = 2 if (width // step) % 2 == 0 else 1
-    length = width // parts
-    starts = range(0, width, length)
+    halves = 2 if width // 128 % 2 == 0 else 1
+    length = width // halves
+    per_half = 2 if length // 128 % 2 == 0 else 1
+    piece = length // per_half
+    step = width_step(piece)
+    parts = [slice(first, first + length) for first in range(0, width, length)]
+
+    def crossed(blocks):
+        came = [to_group(blocks[k - 1], k) for k in range(1, groups)]
+        return came[0] if groups == 2 else jnp.concatenate(came, axis=1)
+
+    def returned_rows(rows, send=to_group):
+        blocks = [
+            send(rows[(k - 1) * capacity : k * capacity], groups - k) for k in range(1, groups)
+        ]
+        return blocks[0] if groups == 2 else jnp.concatenate(blocks, axis=0)
 
     down_second_other = swapped(down_second[0], 2)
     up_first_other = swapped(up_first[0], 1)
@@ -369,20 +416,16 @@
         gain_second,
         grad_second[0],
     )
-
-    def crossed(blocks):
-        came = [to_group(blocks[k - 1], k) for k in range(1, groups)]
-        return came[0] if groups == 2 else jnp.concatenate(came, axis=1)
-
+    notes = jnp.concatenate([routes[0].astype(jnp.float32), weights[0]])
+    notes = shifted(after(notes, up_first_other), "pipe", 1)
     came_second = crossed(cross_second)
     stay_second_other = swapped(after(stay_second, up_first_other), 1)
     up_second_other = swapped(after(up_second[0], up_first_other), 2)
+    down_first_other = swapped(after(down_first[0], up_first_other), 1)
+    came_second = after(came_second, down_second_other, stay_second_other, notes)
+    came_second_other = swapped(came_second, 1)
     came_first = crossed(after(cross_first, up_second_other))
-    down_first_other = swapped(after(down_first[0], up_first_other), 1)
-    came_second = after(came_second, down_second_other, stay_second_other)
-    came_second_other = swapped(came_second, 1)
     stay_first_other = swapped(after(stay_first, up_second_other), 2)
-    came_first_other = swapped(came_first, 2)
 
     rows = [stay_second, came_second, stay_second_other, came_second_other]
     if capacity % 16:
@@ -399,11 +442,12 @@
         scratch_shapes=[pltpu.VMEM((both, 2 * hidden), jnp.float32)] * 2,
         compiler_params=PARAMS,
     )(*rows, up_second[0], up_second_other, down_second[0], down_second_other)
-    own_second, send_second = spread(
-        back_upper, up_second[0], up_second_other, 0, 0, width, step
-    )
+    own_second, send_second = spread(back_upper, up_second[0], up_second_other, 0, 0, width, step)
     came_part = swapped(send_second[capacity:], 1)
-    stay_part = swapped(send_second[:capacity], 1)
+    stay_part = swapped(after(send_second[:capacity], came_part), 1)
+
+    came_first_other = swapped(came_first, 2)
+
     def first_hidden(rows):
         if capacity % 16:
             rows = [jnp.concatenate(rows, axis=1)]
@@ -421,23 +465,18 @@
     weights_down = (down_first[0], down_first_other, 1)
     stay_hidden = first_hidden([after(stay_first, send_second), stay_first_other])
     stay_own, stay_send = spread(stay_hidden, *weights_down, 0, width, step)
-    stay_first_part = swapped(stay_send, 2)
     back = (own_second[capacity:] + after(came_part, stay_send).astype(jnp.float32)).astype(bf16)
-    returned = [
-        to_group(back[(k - 1) * capacity : k * capacity], groups - k) for k in range(1, groups)
+    returned = returned_rows(back)
+    came_hidden = first_hidden([came_first, came_first_other])
+    spreads = [
+        spread(came_hidden, *weights_down, part.start, length, step) for part in parts
     ]
-    returned = returned[0] if groups == 2 else jnp.concatenate(returned, axis=0)
-    came_hidden = first_hidden([came_first, after(came_first_other, stay_send)])
-    spreads = [spread(came_hidden, *weights_down, first, length, step) for first in starts]
     came_parts = [swapped(send, 2) for _, send in spreads]
-    returned_first = []
-    for (own, _), part in zip(spreads, came_parts):
-        back = (own + part.astype(jnp.float32)).astype(bf16)
-        blocks = [
-            to_group(back[(k - 1) * capacity : k * capacity], groups - k)
-            for k in range(1, groups)
-        ]
-        returned_first.append(blocks[0] if groups == 2 else jnp.concatenate(blocks, axis=0))
+    stay_first_part = swapped(after(stay_send, *came_parts), 2)
+    backs = [
+        (own + part.astype(jnp.float32)).astype(bf16) for (own, _), part in zip(spreads, came_parts)
+    ]
+    returned_first = [returned_rows(rows, to_group_ahead) for rows in backs]
 
     grad_acts = pl.pallas_call(
         functools.partial(finish_second_body, groups, capacity, step),
@@ -456,28 +495,31 @@
         returned,
     )
     next_grad = shifted(grad_acts, "pipe", 1)
-    next_parts = []
-    order = [grad_acts, next_grad]
-    for first, back in zip(starts, returned_first):
-        half = functools.partial(columns_block, length, first // length)
-        mixed = pl.pallas_call(
-            functools.partial(finish_first_body, groups, capacity),
-            grid=(1,),
-            in_specs=[WHOLE] * 2 + [half(tokens), half(capacity), half(capacity), WHOLE],
-            out_specs=WHOLE,
-            out_shape=jax.ShapeDtypeStruct((tokens, length), bf16),
-            compiler_params=PARAMS,
-        )(
-            routes[0],
-            weights[0],
-            after(acts_first[0], order[first > 0]),
-            stay_own,
-            stay_first_part,
-            back,
-        )
-        next_parts.append(shifted(mixed, "pipe", 1))
-    next_first = next_parts[0] if parts == 1 else jnp.concatenate(next_parts, axis=1)
-    return (next_first[None], next_grad[None])
+    stayed = pl.pallas_call(
+        functools.partial(finish_stay_body, groups, capacity, step),
+        in_specs=[WHOLE] * 5,
+        out_specs=[WHOLE] * (halves * per_half),
+        out_shape=[jax.ShapeDtypeStruct((tokens, piece), bf16)] * (halves * per_half),
+        compiler_params=PARAMS,
+    )(routes[0], weights[0], after(acts_first[0], next_grad), stay_own, stay_first_part)
+    stayed = [shifted(part, "pipe", 1) for part in stayed]
+
+    next_first = []
+    for n, (part, rows) in enumerate(zip(parts, returned_first)):
+        pieces = stayed[n * per_half : (n + 1) * per_half]
+        next_first = [
+            pl.pallas_call(
+                functools.partial(finish_came_body, groups, capacity, part, per_half),
+                in_specs=[WHOLE] * (2 + per_half)
+                + [pl.BlockSpec(memory_space=pl.ANY)] * len(next_first),
+                out_specs=pl.BlockSpec(memory_space=pl.ANY),
+                out_shape=jax.ShapeDtypeStruct((tokens, width), bf16),
+                scratch_shapes=[pltpu.VMEM((tokens, length), bf16), pltpu.SemaphoreType.DMA],
+                input_output_aliases={2 + per_half: 0} if next_first else {},
+                compiler_params=PARAMS,
+            )(notes, rows, *pieces, *next_first)
+        ]
+    return (next_first[0][None], next_grad[None])
 
 
 def solution(mesh):

time: 239 us -> 236 us (0.987)
  waiting for transfers between devices: 179 us -> 172 us
  Pallas kernels: 25.2 us -> 27.6 us
    ppermute x5 -> x3, waiting for transfers between devices: 69.6 us -> 43.2 us  [to_group(): lax.ppermute(block, 'expert', [(i, (i + distance * SPLIT) % owners) for i...]
    ppermute x0 -> x2, waiting for transfers between devices: none -> 12.7 us  [to_group_ahead(): return lax.ppermute(block, ('pipe', 'expert'), route)]
    ppermute x3 -> x6, waiting for transfers between devices: 7.89 us -> 12.2 us  [shifted(): return lax.ppermute(block, axis, route)]
    ppermute x0 -> x2, starting transfers between devices: none -> 3.7 us  [to_group_ahead(): return lax.ppermute(block, ('pipe', 'expert'), route)]
    ppermute x3 -> x6, starting transfers between devices: 0.17 us -> 3.13 us  [shifted(): return lax.ppermute(block, axis, route)]
    ppermute x13, waiting for transfers between devices: 101 us -> 104 us  [swapped(): lax.ppermute(block, 'expert', [(i, i ^ bit) for i in range(lax.axis_size(...]
    ppermute x5 -> x3, starting transfers between devices: 10.5 us -> 7.91 us  [to_group(): lax.ppermute(block, 'expert', [(i, (i + distance * SPLIT) % owners) for i...]
  transfers between devices with their start and end apart: 21 -> 24, of which waited for: 11 -> 12; matrix products, arithmetic and copies ran while one was open for 0% -> 0% of each run, Pallas kernels for 11% -> 11%
where the time goes in v3:
time: 236 us
  waiting for transfers between devices  172 us (73%)
  starting transfers between devices  29.9 us (13%)
  Pallas kernels  27.6 us (12%)
  local copies, waits for them, and re-layouts  5.41 us (2%)
    ppermute x13, waiting for transfers between devices, swapped(): lax.ppermute(block, 'expert', [(i, i ^ bit) for i in range(lax.axis_size(...  104 us
    ppermute x3, waiting for transfers between devices, to_group(): lax.ppermute(block, 'expert', [(i, (i + distance * SPLIT) % owners) for i...  43.2 us
    ppermute x13, starting transfers between devices, swapped(): lax.ppermute(block, 'expert', [(i, i ^ bit) for i in range(lax.axis_size(...  15.2 us
    ppermute x2, waiting for transfers between devices, to_group_ahead(): return lax.ppermute(block, ('pipe', 'expert'), route)  12.7 us
    ppermute x6, waiting for transfers between devices, shifted(): return lax.ppermute(block, axis, route)  12.2 us
    ppermute x3, starting transfers between devices, to_group(): lax.ppermute(block, 'expert', [(i, (i + distance * SPLIT) % owners) for i...  7.91 us
    pallas_call x4, Pallas kernels, spread(): pl.pallas_call(functools.partial(spread_body, weights_dim, own_rows), gri...  6.86 us
    pallas_call x1, Pallas kernels, per_device(): pl.pallas_call(functools.partial(backward_hidden_body, len(rows)), grid=(...  6.34 us
  transfers between devices with their start and end apart: 24, of which 12 were waited for; matrix products, arithmetic and copies ran while one was open for 0% of the time, Pallas kernels for 11%

profile of v3, /device:TPU:0, one launch (start us, length us, event | category | flops | bytes accessed | tf_op | source)
XLA Modules:
  0.0 236.0 jit_solution(3833997303534582246)
XLA Ops:
  0.6 3.0 %collective-permute-start = (bf16[3584,256]{1,0:T(8,128)(2,1)}, bf16[3584,256]{1,0:T(8,128)(2,1)S(1)}, u32[]{:S(2)}, u32[]{:S(2)}) collective-permute-start(bf16[3584,256]{1,0:T(8,128)(2,1)} %bitcast.20), channel_id=1, source_target_pairs={{0,1},{1,0},{2,3},{3,2},{4,5},{5,4},{6,7},{7,6},{8,9},{9,8},{10,11... | collective-permute-start | bytes 5505032 | tf_op jit(solution)/shard_map/ppermute | solution.py:34
  5.2 5.4 %shard_map.140 = (bf16[1,96,3584]{2,1,0:T(8,128)(2,1)}, bf16[2,96,3584]{2,1,0:T(8,128)(2,1)}, bf16[1,1,96,3584]{3,2,1,0:T(8,128)(2,1)}, bf16[1,2,96,3584]{3,2,1,0:T(8,128)(2,1)}) custom-call(s32[1,128]{1,0:T(1,128)} %bitcast.38, s32[1,128]{1,0:T(1,128)} %bitcast.34, f32[1,128]{1,0:T(1,128)} %bitcast.42, bf16[128,3584]{1,0:T(8,128)(2,1)} %bitcast.30, ...), custom_call_target="tpu_custom_call" | custom-call | tf_op jit(solution)/shard_map/pallas_call | solution.py:170
  10.6 2.7 %collective-permute-start.8 = (bf16[2,96,3584]{2,1,0:T(8,128)(2,1)}, bf16[2,96,3584]{2,1,0:T(8,128)(2,1)S(1)}, u32[]{:S(2)}, u32[]{:S(2)}) collective-permute-start(bf16[2,96,3584]{2,1,0:T(8,128)(2,1)} %bitcast.43), channel_id=1, source_target_pairs={{0,4},{1,5},{2,6},{3,7},{4,0},{5,1},{6,2},{7,3},{8,12},{9,13},{10,... | collective-permute-start | bytes 4128776 | tf_op jit(solution)/shard_map/ppermute | solution.py:43
  13.2 30.6 %collective-permute-done.refs_3_ = bf16[3584,256]{1,0:T(8,128)(2,1)S(1)} collective-permute-done((bf16[3584,256]{1,0:T(8,128)(2,1)}, bf16[3584,256]{1,0:T(8,128)(2,1)S(1)}, u32[]{:S(2)}, u32[]{:S(2)}) %collective-permute-start) | collective-permute-done | bytes 1835040 | tf_op jit(solution)/shard_map/ppermute | solution.py:34
  43.9 1.7 collective-permute-start.10
  47.3 28.2 %collective-permute-done.8.refs_1_ = bf16[2,96,3584]{2,1,0:T(8,128)(2,1)S(1)} collective-permute-done((bf16[2,96,3584]{2,1,0:T(8,128)(2,1)}, bf16[2,96,3584]{2,1,0:T(8,128)(2,1)S(1)}, u32[]{:S(2)}, u32[]{:S(2)}) %collective-permute-start.8) | collective-permute-done | bytes 1376288 | tf_op jit(solution)/shard_map/ppermute | solution.py:43
  78.4 35.7 %collective-permute-done.2.refs_5_.other_ref = bf16[3584,256]{1,0:T(8,128)(2,1)S(1)} collective-permute-done((bf16[3584,256]{1,0:T(8,128)(2,1)}, bf16[3584,256]{1,0:T(8,128)(2,1)S(1)}, u32[]{:S(2)}, u32[]{:S(2)}) %collective-permute-start.2) | collective-permute-done | bytes 1835040 | tf_op jit(solution)/shard_map/ppermute | solution.py:34
  115.7 2.6 %collective-permute-start.3 = (bf16[1,96,3584]{2,1,0:T(8,128)(2,1)}, bf16[1,96,3584]{2,1,0:T(8,128)(2,1)S(1)}, u32[]{:S(2)}, u32[]{:S(2)}) collective-permute-start(bf16[1,96,3584]{2,1,0:T(8,128)(2,1)} %bitcast.44), channel_id=1, source_target_pairs={{0,4},{1,5},{2,6},{3,7},{4,0},{5,1},{6,2},{7,3},{8,12},{9,13},{10,... | collective-permute-start | bytes 2064392 | tf_op jit(solution)/shard_map/ppermute | solution.py:43
  122.6 6.3 %shard_map.143.hidden_ref = bf16[384,512]{1,0:T(8,128)(2,1)S(1)} custom-call(bf16[2,96,3584]{2,1,0:T(8,128)(2,1)S(1)} %copy-done.8, bf16[2,96,3584]{2,1,0:T(8,128)(2,1)S(1)} %collective-permute-done.8.refs_1_, bf16[2,96,3584]{2,1,0:T(8,128)(2,1)S(1)} %collective-permute-done.10.refs_2_, bf16[2,96,3584]{2,1,0:T(8,128)(2,1)S(1)} %collective-permute-done.11.refs_3_, ...), custom_call_target="tpu_custom_call" | custom-call | tf_op jit(solution)/shard_map/pallas_call | solution.py:434
  129.0 2.7 %shard_map.144 = (f32[192,3584]{1,0:T(8,128)S(1)}, bf16[192,3584]{1,0:T(8,128)(2,1)S(1)}) custom-call(bf16[384,512]{1,0:T(8,128)(2,1)S(1)} %shard_map.143.hidden_ref, bf16[3584,256]{1,0:T(8,128)(2,1)S(1)} %bitcast.25, bf16[3584,256]{1,0:T(8,128)(2,1)S(1)} %collective-permute-done.2.refs_5_.other_ref), custom_call_target="tpu_custom_call" | custom-call | tf_op jit(solution)/shard_map/pallas_call | solution.py:251
  132.4 15.0 %collective-permute-done.3.refs_0_ = bf16[1,96,3584]{2,1,0:T(8,128)(2,1)S(1)} collective-permute-done((bf16[1,96,3584]{2,1,0:T(8,128)(2,1)}, bf16[1,96,3584]{2,1,0:T(8,128)(2,1)S(1)}, u32[]{:S(2)}, u32[]{:S(2)}) %collective-permute-start.3) | collective-permute-done | bytes 688160 | tf_op jit(solution)/shard_map/ppermute | solution.py:43
  147.8 1.9 shard_map.145.hidden_ref
  149.7 2.1 shard_map.146
  151.7 9.1 %collective-permute-done.12 = bf16[96,3584]{1,0:T(8,128)(2,1)S(1)} collective-permute-done((bf16[96,3584]{1,0:T(8,128)(2,1)S(1)}, bf16[96,3584]{1,0:T(8,128)(2,1)S(1)}, u32[]{:S(2)}, u32[]{:S(2)}) %collective-permute-start.12) | collective-permute-done | bytes 688160 | tf_op jit(solution)/shard_map/ppermute | solution.py:34
  161.6 2.7 %collective-permute-start.15 = (bf16[96,3584]{1,0:T(8,128)(2,1)S(1)}, bf16[96,3584]{1,0:T(8,128)(2,1)S(1)}, u32[]{:S(2)}, u32[]{:S(2)}) collective-permute-start(bf16[96,3584]{1,0:T(8,128)(2,1)S(1)} %get-tuple-element.58), channel_id=1, source_target_pairs={{0,4},{1,5},{2,6},{3,7},{4,0},{5,1},{6,2},{7,3},{8,12},{9,13},{10,... | collective-permute-start | bytes 2064392 | tf_op jit(solution)/shard_map/ppermute | solution.py:43
  164.2 1.9 shard_map.141.hidden_ref
  167.2 1.6 collective-permute-start.17
  170.4 16.6 %collective-permute-done.17 = bf16[96,1792]{1,0:T(8,128)(2,1)S(1)} collective-permute-done((bf16[96,1792]{1,0:T(8,128)(2,1)S(1)}, bf16[96,1792]{1,0:T(8,128)(2,1)S(1)}, u32[]{:S(2)}, u32[]{:S(2)}) %collective-permute-start.17) | collective-permute-done | bytes 344096 | tf_op jit(solution)/shard_map/ppermute | solution.py:34
  187.0 10.9 %collective-permute-done.6 = bf16[96,1792]{1,0:T(8,128)(2,1)S(1)} collective-permute-done((bf16[96,1792]{1,0:T(8,128)(2,1)S(1)}, bf16[96,1792]{1,0:T(8,128)(2,1)S(1)}, u32[]{:S(2)}, u32[]{:S(2)}) %collective-permute-start.6) | collective-permute-done | bytes 344096 | tf_op jit(solution)/shard_map/ppermute | solution.py:34
  199.8 3.4 %collective-permute-start.21 = (bf16[96,1792]{1,0:T(8,128)(2,1)S(1)}, bf16[96,1792]{1,0:T(8,128)(2,1)S(1)}, u32[]{:S(2)}, u32[]{:S(2)}) collective-permute-start(bf16[96,1792]{1,0:T(8,128)(2,1)S(1)} %add_convert_fusion.1), channel_id=1, source_target_pairs={{0,12},{1,13},{2,14},{3,15},{4,8},{5,9},{6,10},{7,11},{8,20},{9,21... | collective-permute-start | bytes 1032200 | tf_op jit(solution)/shard_map/ppermute | solution.py:24
  203.6 11.8 %collective-permute-done.16 = bf16[128,3584]{1,0:T(8,128)(2,1)S(1)} collective-permute-done((bf16[128,3584]{1,0:T(8,128)(2,1)S(1)}, bf16[128,3584]{1,0:T(8,128)(2,1)S(1)}, u32[]{:S(2)}, u32[]{:S(2)}) %collective-permute-start.16) | collective-permute-done | bytes 917536 | tf_op jit(solution)/shard_map/ppermute | solution.py:30
  217.6 8.4 %collective-permute-done.21.returned_ref = bf16[96,1792]{1,0:T(8,128)(2,1)S(1)} collective-permute-done((bf16[96,1792]{1,0:T(8,128)(2,1)S(1)}, bf16[96,1792]{1,0:T(8,128)(2,1)S(1)}, u32[]{:S(2)}, u32[]{:S(2)}) %collective-permute-start.21) | collective-permute-done | bytes 344096 | tf_op jit(solution)/shard_map/ppermute | solution.py:24
  226.0 1.8 collective-permute-start.20
  229.1 4.2 %collective-permute-done.7.returned_ref = bf16[96,1792]{1,0:T(8,128)(2,1)S(1)} collective-permute-done((bf16[96,1792]{1,0:T(8,128)(2,1)S(1)}, bf16[96,1792]{1,0:T(8,128)(2,1)S(1)}, u32[]{:S(2)}, u32[]{:S(2)}) %collective-permute-start.7) | collective-permute-done | bytes 344096 | tf_op jit(solution)/shard_map/ppermute | solution.py:24
  (71 shorter events, 24.8 us)
Async XLA Ops:
  0.6 43.2 %collective-permute-start = (bf16[3584,256]{1,0:T(8,128)(2,1)}, bf16[3584,256]{1,0:T(8,128)(2,1)S(1)}, u32[]{:S(2)}, u32[]{:S(2)}) collective-permute-start(bf16[3584,256]{1,0:T(8,128)(2,1)} %bitcast.20), channel_id=1, source_target_pairs={{0,1},{1,0},{2,3},{3,2},{4,5},{5,4},{6,7},{7,6},{8,9},{9,8},{10,11... | collective-permute-start | bytes 5505032 | tf_op jit(solution)/shard_map/ppermute | solution.py:34
  3.6 72.7 %collective-permute-start.9 = (bf16[256,3584]{1,0:T(8,128)(2,1)}, bf16[256,3584]{1,0:T(8,128)(2,1)}, u32[]{:S(2)}, u32[]{:S(2)}) collective-permute-start(bf16[256,3584]{1,0:T(8,128)(2,1)} %bitcast.32), channel_id=1, source_target_pairs={{0,2},{1,3},{2,0},{3,1},{4,6},{5,7},{6,4},{7,5},{8,10},{9,11},{10,... | collective-permute-start | bytes 5505032 | tf_op jit(solution)/shard_map/ppermute | solution.py:34
  10.6 64.9 %collective-permute-start.8 = (bf16[2,96,3584]{2,1,0:T(8,128)(2,1)}, bf16[2,96,3584]{2,1,0:T(8,128)(2,1)S(1)}, u32[]{:S(2)}, u32[]{:S(2)}) collective-permute-start(bf16[2,96,3584]{2,1,0:T(8,128)(2,1)} %bitcast.43), channel_id=1, source_target_pairs={{0,4},{1,5},{2,6},{3,7},{4,0},{5,1},{6,2},{7,3},{8,12},{9,13},{10,... | collective-permute-start | bytes 4128776 | tf_op jit(solution)/shard_map/ppermute | solution.py:43
  43.9 32.5 %collective-permute-start.10 = (bf16[2,96,3584]{2,1,0:T(8,128)(2,1)}, bf16[2,96,3584]{2,1,0:T(8,128)(2,1)S(1)}, u32[]{:S(2)}, u32[]{:S(2)}) collective-permute-start(bf16[2,96,3584]{2,1,0:T(8,128)(2,1)} %get-tuple-element.39.refs_0_), channel_id=1, source_target_pairs={{0,1},{1,0},{2,3},{3,2},{4,5},{5,4},{6,7},{7,6},{8,9},{9,8},{10,11... | collective-permute-start | bytes 4128776 | tf_op jit(solution)/shard_map/ppermute | solution.py:34
  45.6 68.5 %collective-permute-start.2 = (bf16[3584,256]{1,0:T(8,128)(2,1)}, bf16[3584,256]{1,0:T(8,128)(2,1)S(1)}, u32[]{:S(2)}, u32[]{:S(2)}) collective-permute-start(bf16[3584,256]{1,0:T(8,128)(2,1)} %bitcast.23), channel_id=1, source_target_pairs={{0,2},{1,3},{2,0},{3,1},{4,6},{5,7},{6,4},{7,5},{8,10},{9,11},{10,... | collective-permute-start | bytes 5505032 | tf_op jit(solution)/shard_map/ppermute | solution.py:34
  47.2 29.2 %collective-permute-start.1 = (f32[2,128]{1,0:T(2,128)S(1)}, f32[2,128]{1,0:T(2,128)S(1)}, u32[]{:S(2)}, u32[]{:S(2)}) collective-permute-start(f32[2,128]{1,0:T(2,128)S(1)} %pad_maximum_fusion), channel_id=1, source_target_pairs={{24,0},{0,8},{8,16},{16,24},{25,1},{1,9},{9,17},{17,25},{26,2},{2,... | collective-permute-start | bytes 3080 | tf_op jit(solution)/shard_map/ppermute | solution.py:30
  76.4 41.9 %collective-permute-start.11 = (bf16[2,96,3584]{2,1,0:T(8,128)(2,1)S(1)}, bf16[2,96,3584]{2,1,0:T(8,128)(2,1)S(1)}, u32[]{:S(2)}, u32[]{:S(2)}) collective-permute-start(bf16[2,96,3584]{2,1,0:T(8,128)(2,1)S(1)} %collective-permute-done.8.refs_1_), channel_id=1, source_target_pairs={{0,1},{1,0},{2,3},{3,2},{4,5},{5,4},{6,7},{7,6},{8,9},{9,8},{10,11... | collective-permute-start | bytes 4128776 | tf_op jit(solution)/shard_map/ppermute | solution.py:34
  77.0 72.7 %collective-permute-start.5 = (bf16[256,3584]{1,0:T(8,128)(2,1)S(1)}, bf16[256,3584]{1,0:T(8,128)(2,1)S(1)}, u32[]{:S(2)}, u32[]{:S(2)}) collective-permute-start(bf16[256,3584]{1,0:T(8,128)(2,1)S(1)} %bitcast.16), channel_id=1, source_target_pairs={{0,1},{1,0},{2,3},{3,2},{4,5},{5,4},{6,7},{7,6},{8,9},{9,8},{10,11... | collective-permute-start | bytes 5505032 | tf_op jit(solution)/shard_map/ppermute | solution.py:34
  114.1 33.6 %collective-permute-start.14 = (bf16[1,96,3584]{2,1,0:T(8,128)(2,1)}, bf16[1,96,3584]{2,1,0:T(8,128)(2,1)S(1)}, u32[]{:S(2)}, u32[]{:S(2)}) collective-permute-start(bf16[1,96,3584]{2,1,0:T(8,128)(2,1)} %get-tuple-element.46.refs_0_), channel_id=1, source_target_pairs={{0,2},{1,3},{2,0},{3,1},{4,6},{5,7},{6,4},{7,5},{8,10},{9,11},{10,... | collective-permute-start | bytes 2064392 | tf_op jit(solution)/shard_map/ppermute | solution.py:34
  115.7 31.7 %collective-permute-start.3 = (bf16[1,96,3584]{2,1,0:T(8,128)(2,1)}, bf16[1,96,3584]{2,1,0:T(8,128)(2,1)S(1)}, u32[]{:S(2)}, u32[]{:S(2)}) collective-permute-start(bf16[1,96,3584]{2,1,0:T(8,128)(2,1)} %bitcast.44), channel_id=1, source_target_pairs={{0,4},{1,5},{2,6},{3,7},{4,0},{5,1},{6,2},{7,3},{8,12},{9,13},{10,... | collective-permute-start | bytes 2064392 | tf_op jit(solution)/shard_map/ppermute | solution.py:43
  131.8 29.0 %collective-permute-start.12 = (bf16[96,3584]{1,0:T(8,128)(2,1)S(1)}, bf16[96,3584]{1,0:T(8,128)(2,1)S(1)}, u32[]{:S(2)}, u32[]{:S(2)}) collective-permute-start(bf16[96,3584]{1,0:T(8,128)(2,1)S(1)} %get-tuple-element.60), channel_id=1, source_target_pairs={{0,1},{1,0},{2,3},{3,2},{4,5},{5,4},{6,7},{7,6},{8,9},{9,8},{10,11... | collective-permute-start | bytes 2064392 | tf_op jit(solution)/shard_map/ppermute | solution.py:34
  147.4 16.8 %collective-permute-start.4 = (bf16[1,96,3584]{2,1,0:T(8,128)(2,1)S(1)}, bf16[1,96,3584]{2,1,0:T(8,128)(2,1)S(1)}, u32[]{:S(2)}, u32[]{:S(2)}) collective-permute-start(bf16[1,96,3584]{2,1,0:T(8,128)(2,1)S(1)} %collective-permute-done.3.refs_0_), channel_id=1, source_target_pairs={{0,2},{1,3},{2,0},{3,1},{4,6},{5,7},{6,4},{7,5},{8,10},{9,11},{10,... | collective-permute-start | bytes 2064392 | tf_op jit(solution)/shard_map/ppermute | solution.py:34
  160.8 37.1 %collective-permute-start.13 = (bf16[96,3584]{1,0:T(8,128)(2,1)S(1)}, bf16[96,3584]{1,0:T(8,128)(2,1)S(1)}, u32[]{:S(2)}, u32[]{:S(2)}) collective-permute-start(bf16[96,3584]{1,0:T(8,128)(2,1)S(1)} %get-tuple-element.43), channel_id=1, source_target_pairs={{0,1},{1,0},{2,3},{3,2},{4,5},{5,4},{6,7},{7,6},{8,9},{9,8},{10,11... | collective-permute-start | bytes 2064392 | tf_op jit(solution)/shard_map/ppermute | solution.py:34
  161.6 36.4 %collective-permute-start.15 = (bf16[96,3584]{1,0:T(8,128)(2,1)S(1)}, bf16[96,3584]{1,0:T(8,128)(2,1)S(1)}, u32[]{:S(2)}, u32[]{:S(2)}) collective-permute-start(bf16[96,3584]{1,0:T(8,128)(2,1)S(1)} %get-tuple-element.58), channel_id=1, source_target_pairs={{0,4},{1,5},{2,6},{3,7},{4,0},{5,1},{6,2},{7,3},{8,12},{9,13},{10,... | collective-permute-start | bytes 2064392 | tf_op jit(solution)/shard_map/ppermute | solution.py:43
  167.2 19.8 %collective-permute-start.17 = (bf16[96,1792]{1,0:T(8,128)(2,1)S(1)}, bf16[96,1792]{1,0:T(8,128)(2,1)S(1)}, u32[]{:S(2)}, u32[]{:S(2)}) collective-permute-start(bf16[96,1792]{1,0:T(8,128)(2,1)S(1)} %get-tuple-element.51), channel_id=1, source_target_pairs={{0,2},{1,3},{2,0},{3,1},{4,6},{5,7},{6,4},{7,5},{8,10},{9,11},{10,... | collective-permute-start | bytes 1032200 | tf_op jit(solution)/shard_map/ppermute | solution.py:34
  169.9 28.1 %collective-permute-start.6 = (bf16[96,1792]{1,0:T(8,128)(2,1)S(1)}, bf16[96,1792]{1,0:T(8,128)(2,1)S(1)}, u32[]{:S(2)}, u32[]{:S(2)}) collective-permute-start(bf16[96,1792]{1,0:T(8,128)(2,1)S(1)} %get-tuple-element.36), channel_id=1, source_target_pairs={{0,2},{1,3},{2,0},{3,1},{4,6},{5,7},{6,4},{7,5},{8,10},{9,11},{10,... | collective-permute-start | bytes 1032200 | tf_op jit(solution)/shard_map/ppermute | solution.py:34
  197.9 17.4 %collective-permute-start.18 = (bf16[96,3584]{1,0:T(8,128)(2,1)S(1)}, bf16[96,3584]{1,0:T(8,128)(2,1)S(1)}, u32[]{:S(2)}, u32[]{:S(2)}) collective-permute-start(bf16[96,3584]{1,0:T(8,128)(2,1)S(1)} %get-tuple-element.52), channel_id=1, source_target_pairs={{0,2},{1,3},{2,0},{3,1},{4,6},{5,7},{6,4},{7,5},{8,10},{9,11},{10,... | collective-permute-start | bytes 2064392 | tf_op jit(solution)/shard_map/ppermute | solution.py:34
  199.6 15.7 %collective-permute-start.16 = (bf16[128,3584]{1,0:T(8,128)(2,1)S(1)}, bf16[128,3584]{1,0:T(8,128)(2,1)S(1)}, u32[]{:S(2)}, u32[]{:S(2)}) collective-permute-start(bf16[128,3584]{1,0:T(8,128)(2,1)S(1)} %shard_map.147), channel_id=1, source_target_pairs={{24,0},{0,8},{8,16},{16,24},{25,1},{1,9},{9,17},{17,25},{26,2},{2,... | collective-permute-start | bytes 2752520 | tf_op jit(solution)/shard_map/ppermute | solution.py:30
  199.8 26.2 %collective-permute-start.21 = (bf16[96,1792]{1,0:T(8,128)(2,1)S(1)}, bf16[96,1792]{1,0:T(8,128)(2,1)S(1)}, u32[]{:S(2)}, u32[]{:S(2)}) collective-permute-start(bf16[96,1792]{1,0:T(8,128)(2,1)S(1)} %add_convert_fusion.1), channel_id=1, source_target_pairs={{0,12},{1,13},{2,14},{3,15},{4,8},{5,9},{6,10},{7,11},{8,20},{9,21... | collective-permute-start | bytes 1032200 | tf_op jit(solution)/shard_map/ppermute | solution.py:24
  203.3 30.1 %collective-permute-start.7 = (bf16[96,1792]{1,0:T(8,128)(2,1)S(1)}, bf16[96,1792]{1,0:T(8,128)(2,1)S(1)}, u32[]{:S(2)}, u32[]{:S(2)}) collective-permute-start(bf16[96,1792]{1,0:T(8,128)(2,1)S(1)} %add_convert_fusion.2), channel_id=1, source_target_pairs={{0,12},{1,13},{2,14},{3,15},{4,8},{5,9},{6,10},{7,11},{8,20},{9,21... | collective-permute-start | bytes 1032200 | tf_op jit(solution)/shard_map/ppermute | solution.py:24
  216.3 11.4 %collective-permute-start.22 = (bf16[128,896]{1,0:T(8,128)(2,1)S(1)}, bf16[128,896]{1,0:T(8,128)(2,1)S(1)}, u32[]{:S(2)}, u32[]{:S(2)}) collective-permute-start(bf16[128,896]{1,0:T(8,128)(2,1)S(1)} %get-tuple-element.56), channel_id=1, source_target_pairs={{24,0},{0,8},{8,16},{16,24},{25,1},{1,9},{9,17},{17,25},{26,2},{2,... | collective-permute-start | bytes 688136 | tf_op jit(solution)/shard_map/ppermute | solution.py:30
  216.4 11.4 %collective-permute-start.23 = (bf16[128,896]{1,0:T(8,128)(2,1)S(1)}, bf16[128,896]{1,0:T(8,128)(2,1)S(1)}, u32[]{:S(2)}, u32[]{:S(2)}) collective-permute-start(bf16[128,896]{1,0:T(8,128)(2,1)S(1)} %get-tuple-element.57), channel_id=1, source_target_pairs={{24,0},{0,8},{8,16},{16,24},{25,1},{1,9},{9,17},{17,25},{26,2},{2,... | collective-permute-start | bytes 688136 | tf_op jit(solution)/shard_map/ppermute | solution.py:30
  217.5 15.9 %collective-permute-start.19 = (bf16[128,896]{1,0:T(8,128)(2,1)S(1)}, bf16[128,896]{1,0:T(8,128)(2,1)S(1)}, u32[]{:S(2)}, u32[]{:S(2)}) collective-permute-start(bf16[128,896]{1,0:T(8,128)(2,1)S(1)} %get-tuple-element.53), channel_id=1, source_target_pairs={{24,0},{0,8},{8,16},{16,24},{25,1},{1,9},{9,17},{17,25},{26,2},{2,... | collective-permute-start | bytes 688136 | tf_op jit(solution)/shard_map/ppermute | solution.py:30
  226.0 7.7 %collective-permute-start.20 = (bf16[128,896]{1,0:T(8,128)(2,1)S(1)}, bf16[128,896]{1,0:T(8,128)(2,1)S(1)}, u32[]{:S(2)}, u32[]{:S(2)}) collective-permute-start(bf16[128,896]{1,0:T(8,128)(2,1)S(1)} %get-tuple-element.54), channel_id=1, source_target_pairs={{24,0},{0,8},{8,16},{16,24},{25,1},{1,9},{9,17},{17,25},{26,2},{2,... | collective-permute-start | bytes 688136 | tf_op jit(solution)/shard_map/ppermute | solution.py:30
  (14 other events, 337.3 us)

commit v4 on v3

--- a/solution.py
+++ b/solution.py
@@ -444,7 +444,7 @@
     )(*rows, up_second[0], up_second_other, down_second[0], down_second_other)
     own_second, send_second = spread(back_upper, up_second[0], up_second_other, 0, 0, width, step)
     came_part = swapped(send_second[capacity:], 1)
-    stay_part = swapped(after(send_second[:capacity], came_part), 1)
+    stay_part = swapped(send_second[:capacity], 1)
 
     came_first_other = swapped(came_first, 2)
 

time: 236 us -> 235 us (level)
    ppermute x13, waiting for transfers between devices: 104 us -> 101 us  [swapped(): lax.ppermute(block, 'expert', [(i, i ^ bit) for i in range(lax.axis_size(...]
where the time goes in v4:
time: 235 us
  waiting for transfers between devices  170 us (72%)
  starting transfers between devices  31 us (13%)
  Pallas kernels  27.6 us (12%)
  local copies, waits for them, and re-layouts  5.41 us (2%)
    ppermute x13, waiting for transfers between devices, swapped(): lax.ppermute(block, 'expert', [(i, i ^ bit) for i in range(lax.axis_size(...  101 us
    ppermute x3, waiting for transfers between devices, to_group(): lax.ppermute(block, 'expert', [(i, (i + distance * SPLIT) % owners) for i...  43.2 us
    ppermute x13, starting transfers between devices, swapped(): lax.ppermute(block, 'expert', [(i, i ^ bit) for i in range(lax.axis_size(...  16.9 us
    ppermute x2, waiting for transfers between devices, to_group_ahead(): return lax.ppermute(block, ('pipe', 'expert'), route)  13.3 us
    ppermute x6, waiting for transfers between devices, shifted(): return lax.ppermute(block, axis, route)  12.2 us
    ppermute x3, starting transfers between devices, to_group(): lax.ppermute(block, 'expert', [(i, (i + distance * SPLIT) % owners) for i...  7.76 us
    pallas_call x4, Pallas kernels, spread(): pl.pallas_call(functools.partial(spread_body, weights_dim, own_rows), gri...  6.91 us
    pallas_call x1, Pallas kernels, per_device(): pl.pallas_call(functools.partial(backward_hidden_body, len(rows)), grid=(...  6.32 us
  transfers between devices with their start and end apart: 24, of which 12 were waited for; matrix products, arithmetic and copies ran while one was open for 0% of the time, Pallas kernels for 11%

profile of v4, /device:TPU:0, one launch (start us, length us, event | category | flops | bytes accessed | tf_op | source)
XLA Modules:
  0.0 234.9 jit_solution(375663548294919102)
XLA Ops:
  0.6 3.0 %collective-permute-start = (bf16[3584,256]{1,0:T(8,128)(2,1)}, bf16[3584,256]{1,0:T(8,128)(2,1)S(1)}, u32[]{:S(2)}, u32[]{:S(2)}) collective-permute-start(bf16[3584,256]{1,0:T(8,128)(2,1)} %bitcast.20), channel_id=1, source_target_pairs={{0,1},{1,0},{2,3},{3,2},{4,5},{5,4},{6,7},{7,6},{8,9},{9,8},{10,11... | collective-permute-start | bytes 5505032 | tf_op jit(solution)/shard_map/ppermute | solution.py:34
  5.2 5.4 %shard_map.140 = (bf16[1,96,3584]{2,1,0:T(8,128)(2,1)}, bf16[2,96,3584]{2,1,0:T(8,128)(2,1)}, bf16[1,1,96,3584]{3,2,1,0:T(8,128)(2,1)}, bf16[1,2,96,3584]{3,2,1,0:T(8,128)(2,1)}) custom-call(s32[1,128]{1,0:T(1,128)} %bitcast.38, s32[1,128]{1,0:T(1,128)} %bitcast.34, f32[1,128]{1,0:T(1,128)} %bitcast.42, bf16[128,3584]{1,0:T(8,128)(2,1)} %bitcast.30, ...), custom_call_target="tpu_custom_call" | custom-call | tf_op jit(solution)/shard_map/pallas_call | solution.py:170
  10.6 2.7 %collective-permute-start.8 = (bf16[2,96,3584]{2,1,0:T(8,128)(2,1)}, bf16[2,96,3584]{2,1,0:T(8,128)(2,1)S(1)}, u32[]{:S(2)}, u32[]{:S(2)}) collective-permute-start(bf16[2,96,3584]{2,1,0:T(8,128)(2,1)} %bitcast.43), channel_id=1, source_target_pairs={{0,4},{1,5},{2,6},{3,7},{4,0},{5,1},{6,2},{7,3},{8,12},{9,13},{10,... | collective-permute-start | bytes 4128776 | tf_op jit(solution)/shard_map/ppermute | solution.py:43
  13.2 30.6 %collective-permute-done.refs_3_ = bf16[3584,256]{1,0:T(8,128)(2,1)S(1)} collective-permute-done((bf16[3584,256]{1,0:T(8,128)(2,1)}, bf16[3584,256]{1,0:T(8,128)(2,1)S(1)}, u32[]{:S(2)}, u32[]{:S(2)}) %collective-permute-start) | collective-permute-done | bytes 1835040 | tf_op jit(solution)/shard_map/ppermute | solution.py:34
  43.9 1.7 collective-permute-start.10
  47.3 28.2 %collective-permute-done.8.refs_1_ = bf16[2,96,3584]{2,1,0:T(8,128)(2,1)S(1)} collective-permute-done((bf16[2,96,3584]{2,1,0:T(8,128)(2,1)}, bf16[2,96,3584]{2,1,0:T(8,128)(2,1)S(1)}, u32[]{:S(2)}, u32[]{:S(2)}) %collective-permute-start.8) | collective-permute-done | bytes 1376288 | tf_op jit(solution)/shard_map/ppermute | solution.py:43
  78.4 35.7 %collective-permute-done.2.refs_5_.other_ref = bf16[3584,256]{1,0:T(8,128)(2,1)S(1)} collective-permute-done((bf16[3584,256]{1,0:T(8,128)(2,1)}, bf16[3584,256]{1,0:T(8,128)(2,1)S(1)}, u32[]{:S(2)}, u32[]{:S(2)}) %collective-permute-start.2) | collective-permute-done | bytes 1835040 | tf_op jit(solution)/shard_map/ppermute | solution.py:34
  115.7 2.6 %collective-permute-start.3 = (bf16[1,96,3584]{2,1,0:T(8,128)(2,1)}, bf16[1,96,3584]{2,1,0:T(8,128)(2,1)S(1)}, u32[]{:S(2)}, u32[]{:S(2)}) collective-permute-start(bf16[1,96,3584]{2,1,0:T(8,128)(2,1)} %bitcast.44), channel_id=1, source_target_pairs={{0,4},{1,5},{2,6},{3,7},{4,0},{5,1},{6,2},{7,3},{8,12},{9,13},{10,... | collective-permute-start | bytes 2064392 | tf_op jit(solution)/shard_map/ppermute | solution.py:43
  122.6 6.3 %shard_map.143.hidden_ref = bf16[384,512]{1,0:T(8,128)(2,1)S(1)} custom-call(bf16[2,96,3584]{2,1,0:T(8,128)(2,1)S(1)} %copy-done.8, bf16[2,96,3584]{2,1,0:T(8,128)(2,1)S(1)} %collective-permute-done.8.refs_1_, bf16[2,96,3584]{2,1,0:T(8,128)(2,1)S(1)} %collective-permute-done.10.refs_2_, bf16[2,96,3584]{2,1,0:T(8,128)(2,1)S(1)} %collective-permute-done.11.refs_3_, ...), custom_call_target="tpu_custom_call" | custom-call | tf_op jit(solution)/shard_map/pallas_call | solution.py:434
  129.0 2.7 %shard_map.144 = (f32[192,3584]{1,0:T(8,128)S(1)}, bf16[192,3584]{1,0:T(8,128)(2,1)S(1)}) custom-call(bf16[384,512]{1,0:T(8,128)(2,1)S(1)} %shard_map.143.hidden_ref, bf16[3584,256]{1,0:T(8,128)(2,1)S(1)} %bitcast.25, bf16[3584,256]{1,0:T(8,128)(2,1)S(1)} %collective-permute-done.2.refs_5_.other_ref), custom_call_target="tpu_custom_call" | custom-call | tf_op jit(solution)/shard_map/pallas_call | solution.py:251
  132.4 15.0 %collective-permute-done.3.refs_0_ = bf16[1,96,3584]{2,1,0:T(8,128)(2,1)S(1)} collective-permute-done((bf16[1,96,3584]{2,1,0:T(8,128)(2,1)}, bf16[1,96,3584]{2,1,0:T(8,128)(2,1)S(1)}, u32[]{:S(2)}, u32[]{:S(2)}) %collective-permute-start.3) | collective-permute-done | bytes 688160 | tf_op jit(solution)/shard_map/ppermute | solution.py:43
  148.3 1.9 shard_map.145.hidden_ref
  150.2 2.1 shard_map.146
  152.3 11.3 %collective-permute-done.13 = bf16[96,3584]{1,0:T(8,128)(2,1)S(1)} collective-permute-done((bf16[96,3584]{1,0:T(8,128)(2,1)S(1)}, bf16[96,3584]{1,0:T(8,128)(2,1)S(1)}, u32[]{:S(2)}, u32[]{:S(2)}) %collective-permute-start.13) | collective-permute-done | bytes 688160 | tf_op jit(solution)/shard_map/ppermute | solution.py:34
  163.8 2.5 %collective-permute-start.15 = (bf16[96,3584]{1,0:T(8,128)(2,1)S(1)}, bf16[96,3584]{1,0:T(8,128)(2,1)S(1)}, u32[]{:S(2)}, u32[]{:S(2)}) collective-permute-start(bf16[96,3584]{1,0:T(8,128)(2,1)S(1)} %get-tuple-element.56), channel_id=1, source_target_pairs={{0,4},{1,5},{2,6},{3,7},{4,0},{5,1},{6,2},{7,3},{8,12},{9,13},{10,... | collective-permute-start | bytes 2064392 | tf_op jit(solution)/shard_map/ppermute | solution.py:43
  166.3 1.8 shard_map.141.hidden_ref
  169.3 1.8 collective-permute-start.17
  172.5 14.3 %collective-permute-done.17 = bf16[96,1792]{1,0:T(8,128)(2,1)S(1)} collective-permute-done((bf16[96,1792]{1,0:T(8,128)(2,1)S(1)}, bf16[96,1792]{1,0:T(8,128)(2,1)S(1)}, u32[]{:S(2)}, u32[]{:S(2)}) %collective-permute-start.17) | collective-permute-done | bytes 344096 | tf_op jit(solution)/shard_map/ppermute | solution.py:34
  186.8 8.1 %collective-permute-done.6 = bf16[96,1792]{1,0:T(8,128)(2,1)S(1)} collective-permute-done((bf16[96,1792]{1,0:T(8,128)(2,1)S(1)}, bf16[96,1792]{1,0:T(8,128)(2,1)S(1)}, u32[]{:S(2)}, u32[]{:S(2)}) %collective-permute-start.6) | collective-permute-done | bytes 344096 | tf_op jit(solution)/shard_map/ppermute | solution.py:34
  194.8 1.8 collective-permute-start.18
  198.5 2.3 collective-permute-start.21
  202.2 11.9 %collective-permute-done.16 = bf16[128,3584]{1,0:T(8,128)(2,1)S(1)} collective-permute-done((bf16[128,3584]{1,0:T(8,128)(2,1)S(1)}, bf16[128,3584]{1,0:T(8,128)(2,1)S(1)}, u32[]{:S(2)}, u32[]{:S(2)}) %collective-permute-start.16) | collective-permute-done | bytes 917536 | tf_op jit(solution)/shard_map/ppermute | solution.py:30
  216.5 8.4 %collective-permute-done.21.returned_ref = bf16[96,1792]{1,0:T(8,128)(2,1)S(1)} collective-permute-done((bf16[96,1792]{1,0:T(8,128)(2,1)S(1)}, bf16[96,1792]{1,0:T(8,128)(2,1)S(1)}, u32[]{:S(2)}, u32[]{:S(2)}) %collective-permute-start.21) | collective-permute-done | bytes 344096 | tf_op jit(solution)/shard_map/ppermute | solution.py:24
  227.4 4.9 %collective-permute-done.7.returned_ref = bf16[96,1792]{1,0:T(8,128)(2,1)S(1)} collective-permute-done((bf16[96,1792]{1,0:T(8,128)(2,1)S(1)}, bf16[96,1792]{1,0:T(8,128)(2,1)S(1)}, u32[]{:S(2)}, u32[]{:S(2)}) %collective-permute-start.7) | collective-permute-done | bytes 344096 | tf_op jit(solution)/shard_map/ppermute | solution.py:24
  (71 shorter events, 27.0 us)
Async XLA Ops:
  0.6 43.2 %collective-permute-start = (bf16[3584,256]{1,0:T(8,128)(2,1)}, bf16[3584,256]{1,0:T(8,128)(2,1)S(1)}, u32[]{:S(2)}, u32[]{:S(2)}) collective-permute-start(bf16[3584,256]{1,0:T(8,128)(2,1)} %bitcast.20), channel_id=1, source_target_pairs={{0,1},{1,0},{2,3},{3,2},{4,5},{5,4},{6,7},{7,6},{8,9},{9,8},{10,11... | collective-permute-start | bytes 5505032 | tf_op jit(solution)/shard_map/ppermute | solution.py:34
  3.6 72.7 %collective-permute-start.9 = (bf16[256,3584]{1,0:T(8,128)(2,1)}, bf16[256,3584]{1,0:T(8,128)(2,1)}, u32[]{:S(2)}, u32[]{:S(2)}) collective-permute-start(bf16[256,3584]{1,0:T(8,128)(2,1)} %bitcast.32), channel_id=1, source_target_pairs={{0,2},{1,3},{2,0},{3,1},{4,6},{5,7},{6,4},{7,5},{8,10},{9,11},{10,... | collective-permute-start | bytes 5505032 | tf_op jit(solution)/shard_map/ppermute | solution.py:34
  10.6 64.9 %collective-permute-start.8 = (bf16[2,96,3584]{2,1,0:T(8,128)(2,1)}, bf16[2,96,3584]{2,1,0:T(8,128)(2,1)S(1)}, u32[]{:S(2)}, u32[]{:S(2)}) collective-permute-start(bf16[2,96,3584]{2,1,0:T(8,128)(2,1)} %bitcast.43), channel_id=1, source_target_pairs={{0,4},{1,5},{2,6},{3,7},{4,0},{5,1},{6,2},{7,3},{8,12},{9,13},{10,... | collective-permute-start | bytes 4128776 | tf_op jit(solution)/shard_map/ppermute | solution.py:43
  43.9 32.5 %collective-permute-start.10 = (bf16[2,96,3584]{2,1,0:T(8,128)(2,1)}, bf16[2,96,3584]{2,1,0:T(8,128)(2,1)S(1)}, u32[]{:S(2)}, u32[]{:S(2)}) collective-permute-start(bf16[2,96,3584]{2,1,0:T(8,128)(2,1)} %get-tuple-element.38.refs_0_), channel_id=1, source_target_pairs={{0,1},{1,0},{2,3},{3,2},{4,5},{5,4},{6,7},{7,6},{8,9},{9,8},{10,11... | collective-permute-start | bytes 4128776 | tf_op jit(solution)/shard_map/ppermute | solution.py:34
  45.6 68.5 %collective-permute-start.2 = (bf16[3584,256]{1,0:T(8,128)(2,1)}, bf16[3584,256]{1,0:T(8,128)(2,1)S(1)}, u32[]{:S(2)}, u32[]{:S(2)}) collective-permute-start(bf16[3584,256]{1,0:T(8,128)(2,1)} %bitcast.23), channel_id=1, source_target_pairs={{0,2},{1,3},{2,0},{3,1},{4,6},{5,7},{6,4},{7,5},{8,10},{9,11},{10,... | collective-permute-start | bytes 5505032 | tf_op jit(solution)/shard_map/ppermute | solution.py:34
  47.2 29.2 %collective-permute-start.1 = (f32[2,128]{1,0:T(2,128)S(1)}, f32[2,128]{1,0:T(2,128)S(1)}, u32[]{:S(2)}, u32[]{:S(2)}) collective-permute-start(f32[2,128]{1,0:T(2,128)S(1)} %pad_maximum_fusion), channel_id=1, source_target_pairs={{24,0},{0,8},{8,16},{16,24},{25,1},{1,9},{9,17},{17,25},{26,2},{2,... | collective-permute-start | bytes 3080 | tf_op jit(solution)/shard_map/ppermute | solution.py:30
  76.4 41.9 %collective-permute-start.11 = (bf16[2,96,3584]{2,1,0:T(8,128)(2,1)S(1)}, bf16[2,96,3584]{2,1,0:T(8,128)(2,1)S(1)}, u32[]{:S(2)}, u32[]{:S(2)}) collective-permute-start(bf16[2,96,3584]{2,1,0:T(8,128)(2,1)S(1)} %collective-permute-done.8.refs_1_), channel_id=1, source_target_pairs={{0,1},{1,0},{2,3},{3,2},{4,5},{5,4},{6,7},{7,6},{8,9},{9,8},{10,11... | collective-permute-start | bytes 4128776 | tf_op jit(solution)/shard_map/ppermute | solution.py:34
  77.0 73.2 %collective-permute-start.5 = (bf16[256,3584]{1,0:T(8,128)(2,1)S(1)}, bf16[256,3584]{1,0:T(8,128)(2,1)S(1)}, u32[]{:S(2)}, u32[]{:S(2)}) collective-permute-start(bf16[256,3584]{1,0:T(8,128)(2,1)S(1)} %bitcast.16), channel_id=1, source_target_pairs={{0,1},{1,0},{2,3},{3,2},{4,5},{5,4},{6,7},{7,6},{8,9},{9,8},{10,11... | collective-permute-start | bytes 5505032 | tf_op jit(solution)/shard_map/ppermute | solution.py:34
  114.1 34.2 %collective-permute-start.14 = (bf16[1,96,3584]{2,1,0:T(8,128)(2,1)}, bf16[1,96,3584]{2,1,0:T(8,128)(2,1)S(1)}, u32[]{:S(2)}, u32[]{:S(2)}) collective-permute-start(bf16[1,96,3584]{2,1,0:T(8,128)(2,1)} %get-tuple-element.44.refs_0_), channel_id=1, source_target_pairs={{0,2},{1,3},{2,0},{3,1},{4,6},{5,7},{6,4},{7,5},{8,10},{9,11},{10,... | collective-permute-start | bytes 2064392 | tf_op jit(solution)/shard_map/ppermute | solution.py:34
  115.7 31.7 %collective-permute-start.3 = (bf16[1,96,3584]{2,1,0:T(8,128)(2,1)}, bf16[1,96,3584]{2,1,0:T(8,128)(2,1)S(1)}, u32[]{:S(2)}, u32[]{:S(2)}) collective-permute-start(bf16[1,96,3584]{2,1,0:T(8,128)(2,1)} %bitcast.44), channel_id=1, source_target_pairs={{0,4},{1,5},{2,6},{3,7},{4,0},{5,1},{6,2},{7,3},{8,12},{9,13},{10,... | collective-permute-start | bytes 2064392 | tf_op jit(solution)/shard_map/ppermute | solution.py:43
  131.8 31.7 %collective-permute-start.13 = (bf16[96,3584]{1,0:T(8,128)(2,1)S(1)}, bf16[96,3584]{1,0:T(8,128)(2,1)S(1)}, u32[]{:S(2)}, u32[]{:S(2)}) collective-permute-start(bf16[96,3584]{1,0:T(8,128)(2,1)S(1)} %get-tuple-element.58), channel_id=1, source_target_pairs={{0,1},{1,0},{2,3},{3,2},{4,5},{5,4},{6,7},{7,6},{8,9},{9,8},{10,11... | collective-permute-start | bytes 2064392 | tf_op jit(solution)/shard_map/ppermute | solution.py:34
  147.4 18.8 %collective-permute-start.4 = (bf16[1,96,3584]{2,1,0:T(8,128)(2,1)S(1)}, bf16[1,96,3584]{2,1,0:T(8,128)(2,1)S(1)}, u32[]{:S(2)}, u32[]{:S(2)}) collective-permute-start(bf16[1,96,3584]{2,1,0:T(8,128)(2,1)S(1)} %collective-permute-done.3.refs_0_), channel_id=1, source_target_pairs={{0,2},{1,3},{2,0},{3,1},{4,6},{5,7},{6,4},{7,5},{8,10},{9,11},{10,... | collective-permute-start | bytes 2064392 | tf_op jit(solution)/shard_map/ppermute | solution.py:34
  147.8 48.9 %collective-permute-start.12 = (bf16[96,3584]{1,0:T(8,128)(2,1)S(1)}, bf16[96,3584]{1,0:T(8,128)(2,1)S(1)}, u32[]{:S(2)}, u32[]{:S(2)}) collective-permute-start(bf16[96,3584]{1,0:T(8,128)(2,1)S(1)} %get-tuple-element.59), channel_id=1, source_target_pairs={{0,1},{1,0},{2,3},{3,2},{4,5},{5,4},{6,7},{7,6},{8,9},{9,8},{10,11... | collective-permute-start | bytes 2064392 | tf_op jit(solution)/shard_map/ppermute | solution.py:34
  163.8 32.9 %collective-permute-start.15 = (bf16[96,3584]{1,0:T(8,128)(2,1)S(1)}, bf16[96,3584]{1,0:T(8,128)(2,1)S(1)}, u32[]{:S(2)}, u32[]{:S(2)}) collective-permute-start(bf16[96,3584]{1,0:T(8,128)(2,1)S(1)} %get-tuple-element.56), channel_id=1, source_target_pairs={{0,4},{1,5},{2,6},{3,7},{4,0},{5,1},{6,2},{7,3},{8,12},{9,13},{10,... | collective-permute-start | bytes 2064392 | tf_op jit(solution)/shard_map/ppermute | solution.py:43
  169.3 17.5 %collective-permute-start.17 = (bf16[96,1792]{1,0:T(8,128)(2,1)S(1)}, bf16[96,1792]{1,0:T(8,128)(2,1)S(1)}, u32[]{:S(2)}, u32[]{:S(2)}) collective-permute-start(bf16[96,1792]{1,0:T(8,128)(2,1)S(1)} %get-tuple-element.49), channel_id=1, source_target_pairs={{0,2},{1,3},{2,0},{3,1},{4,6},{5,7},{6,4},{7,5},{8,10},{9,11},{10,... | collective-permute-start | bytes 1032200 | tf_op jit(solution)/shard_map/ppermute | solution.py:34
  172.1 22.7 %collective-permute-start.6 = (bf16[96,1792]{1,0:T(8,128)(2,1)S(1)}, bf16[96,1792]{1,0:T(8,128)(2,1)S(1)}, u32[]{:S(2)}, u32[]{:S(2)}) collective-permute-start(bf16[96,1792]{1,0:T(8,128)(2,1)S(1)} %get-tuple-element.35), channel_id=1, source_target_pairs={{0,2},{1,3},{2,0},{3,1},{4,6},{5,7},{6,4},{7,5},{8,10},{9,11},{10,... | collective-permute-start | bytes 1032200 | tf_op jit(solution)/shard_map/ppermute | solution.py:34
  194.8 19.4 %collective-permute-start.18 = (bf16[96,3584]{1,0:T(8,128)(2,1)S(1)}, bf16[96,3584]{1,0:T(8,128)(2,1)S(1)}, u32[]{:S(2)}, u32[]{:S(2)}) collective-permute-start(bf16[96,3584]{1,0:T(8,128)(2,1)S(1)} %get-tuple-element.50), channel_id=1, source_target_pairs={{0,2},{1,3},{2,0},{3,1},{4,6},{5,7},{6,4},{7,5},{8,10},{9,11},{10,... | collective-permute-start | bytes 2064392 | tf_op jit(solution)/shard_map/ppermute | solution.py:34
  198.3 15.9 %collective-permute-start.16 = (bf16[128,3584]{1,0:T(8,128)(2,1)S(1)}, bf16[128,3584]{1,0:T(8,128)(2,1)S(1)}, u32[]{:S(2)}, u32[]{:S(2)}) collective-permute-start(bf16[128,3584]{1,0:T(8,128)(2,1)S(1)} %shard_map.147), channel_id=1, source_target_pairs={{24,0},{0,8},{8,16},{16,24},{25,1},{1,9},{9,17},{17,25},{26,2},{2,... | collective-permute-start | bytes 2752520 | tf_op jit(solution)/shard_map/ppermute | solution.py:30
  198.5 26.5 %collective-permute-start.21 = (bf16[96,1792]{1,0:T(8,128)(2,1)S(1)}, bf16[96,1792]{1,0:T(8,128)(2,1)S(1)}, u32[]{:S(2)}, u32[]{:S(2)}) collective-permute-start(bf16[96,1792]{1,0:T(8,128)(2,1)S(1)} %add_convert_fusion.1), channel_id=1, source_target_pairs={{0,12},{1,13},{2,14},{3,15},{4,8},{5,9},{6,10},{7,11},{8,20},{9,21... | collective-permute-start | bytes 1032200 | tf_op jit(solution)/shard_map/ppermute | solution.py:24
  200.8 31.5 %collective-permute-start.7 = (bf16[96,1792]{1,0:T(8,128)(2,1)S(1)}, bf16[96,1792]{1,0:T(8,128)(2,1)S(1)}, u32[]{:S(2)}, u32[]{:S(2)}) collective-permute-start(bf16[96,1792]{1,0:T(8,128)(2,1)S(1)} %add_convert_fusion.2), channel_id=1, source_target_pairs={{0,12},{1,13},{2,14},{3,15},{4,8},{5,9},{6,10},{7,11},{8,20},{9,21... | collective-permute-start | bytes 1032200 | tf_op jit(solution)/shard_map/ppermute | solution.py:24
  215.2 10.9 %collective-permute-start.22 = (bf16[128,896]{1,0:T(8,128)(2,1)S(1)}, bf16[128,896]{1,0:T(8,128)(2,1)S(1)}, u32[]{:S(2)}, u32[]{:S(2)}) collective-permute-start(bf16[128,896]{1,0:T(8,128)(2,1)S(1)} %get-tuple-element.54), channel_id=1, source_target_pairs={{24,0},{0,8},{8,16},{16,24},{25,1},{1,9},{9,17},{17,25},{26,2},{2,... | collective-permute-start | bytes 688136 | tf_op jit(solution)/shard_map/ppermute | solution.py:30
  215.2 10.8 %collective-permute-start.23 = (bf16[128,896]{1,0:T(8,128)(2,1)S(1)}, bf16[128,896]{1,0:T(8,128)(2,1)S(1)}, u32[]{:S(2)}, u32[]{:S(2)}) collective-permute-start(bf16[128,896]{1,0:T(8,128)(2,1)S(1)} %get-tuple-element.55), channel_id=1, source_target_pairs={{24,0},{0,8},{8,16},{16,24},{25,1},{1,9},{9,17},{17,25},{26,2},{2,... | collective-permute-start | bytes 688136 | tf_op jit(solution)/shard_map/ppermute | solution.py:30
  216.5 15.9 %collective-permute-start.19 = (bf16[128,896]{1,0:T(8,128)(2,1)S(1)}, bf16[128,896]{1,0:T(8,128)(2,1)S(1)}, u32[]{:S(2)}, u32[]{:S(2)}) collective-permute-start(bf16[128,896]{1,0:T(8,128)(2,1)S(1)} %get-tuple-element.51), channel_id=1, source_target_pairs={{24,0},{0,8},{8,16},{16,24},{25,1},{1,9},{9,17},{17,25},{26,2},{2,... | collective-permute-start | bytes 688136 | tf_op jit(solution)/shard_map/ppermute | solution.py:30
  225.0 7.6 %collective-permute-start.20 = (bf16[128,896]{1,0:T(8,128)(2,1)S(1)}, bf16[128,896]{1,0:T(8,128)(2,1)S(1)}, u32[]{:S(2)}, u32[]{:S(2)}) collective-permute-start(bf16[128,896]{1,0:T(8,128)(2,1)S(1)} %get-tuple-element.52), channel_id=1, source_target_pairs={{24,0},{0,8},{8,16},{16,24},{25,1},{1,9},{9,17},{17,25},{26,2},{2,... | collective-permute-start | bytes 688136 | tf_op jit(solution)/shard_map/ppermute | solution.py:30
  (14 other events, 325.0 us)
